TPU v7x, 32 devices: a whole 2x2x4 slice. The times are simulated.
32 devices in a mesh: dp: 8 (over z, y), mp: 4 (over x, core).
Axes of the slice: x: 2, y: 2, z: 4, core: 2. Of those that a mesh axis runs over, the one named last changes fastest.
Arguments:
- latents: bfloat16 [2, 16, 8192], P(None, None, ('dp', 'mp')), may hold values from -6 to 6
- noise: float32 [2, 16, 8192], P(None, None, ('dp', 'mp')), may hold values from -6 to 6
- timesteps: int32 [2, 8], P(None, 'dp'), may hold values from 0 to 999
- labels: int32 [2, 8], P(None, 'dp'), may hold values from 0 to 999
- grid: int32 [2, 2, 8], P(None, None, 'dp'), may hold values from 1 to 32, as said below
- flat_master: float32 [21430656], P(('dp', 'mp'))
- flat_moment: float32 [21430656], P(('dp', 'mp'))
- flat_second: float32 [21430656], P(('dp', 'mp'))
- tile_master: float32 [4, 96, 288, 288], P('mp', 'dp')
- tile_moment: float32 [4, 96, 288, 288], P('mp', 'dp'), may hold values from -9.536743e-06 to 9.536743e-06
- tile_left: float32 [4, 96, 288, 288], P('mp', 'dp')
- tile_right: float32 [4, 96, 288, 288], P('mp', 'dp')
- left_root: float32 [4, 96, 288, 288], P('mp', 'dp')
- right_root: float32 [4, 96, 288, 288], P('mp', 'dp')
Outputs:
- summed_loss: float32 [], replicated
- valid_count: float32 [], replicated
- grad_norm: float32 [], replicated
- flat_new_moment: float32 [21430656], P(('dp', 'mp'))
- flat_new_second: float32 [21430656], P(('dp', 'mp'))
- flat_new_master: float32 [21430656], P(('dp', 'mp'))
- tile_new_moment: float32 [4, 96, 288, 288], P('mp', 'dp')
- tile_new_left: float32 [4, 96, 288, 288], P('mp', 'dp')
- tile_new_right: float32 [4, 96, 288, 288], P('mp', 'dp')
- tile_new_master: float32 [4, 96, 288, 288], P('mp', 'dp')
Inputs may be any that keep to these rules, and one draw needn't show every extreme that they name: `grid`: each latent has 1 to 32 patch rows and 1 to 32 patch columns; in every group one of its 2 latents has 32 rows and more than three quarters of 1024 valid slots.
All inputs are finite; a program needn't handle non-finite values.
Results may differ from a plain program's by a relative error of at most 0.0056.
Values may be sent and summed in bfloat16 or wider, within the bound.
A program may use at most 768 MiB of HBM per device.

v0:
```python
import math

import jax
import jax.numpy as jnp
from jax import lax
from jax.sharding import Mesh
from jax.sharding import PartitionSpec as P

D = 1152
HD = 72
FF = 4608
PATCH = 16
FREQ = 256
CLASSES = 1000
BLK = 288
LAYERS = 2
STEP_COUNT = 10
MB = 2
LANE = 128
STRIP = 3 * BLK


HIGH = lax.Precision.HIGHEST
NORM_EPS = 1e-06
CLIP_AT = 0.005
ADAM_ONE = 0.9
ADAM_TWO = 0.999
ADAM_EPS = 1e-08
ADAM_RATE = 0.02
ADAM_DECAY = 0.01
SHAMPOO_ONE = 0.9
SHAMPOO_TWO = 0.99
SHAMPOO_RATE = 0.01
SHAMPOO_DECAY = 0.01

F32 = jnp.float32
BF16 = jnp.bfloat16
SWAP = [(0, 1), (1, 0)]

ROW_D = D // LANE
ROW_STEM = (PATCH + 1) * ROW_D
BASE_W1 = ROW_STEM
BASE_B1 = BASE_W1 + FREQ * ROW_D
BASE_W2 = BASE_B1 + ROW_D
BASE_B2 = BASE_W2 + D * ROW_D
BASE_TABLE = BASE_B2 + ROW_D
BASE_LAYER = BASE_TABLE + CLASSES * ROW_D
ROW_ADA = 6 * ROW_D
ROW_BIAS = (6 + 3 + 1 + 4 + 1) * ROW_D
LAYER_ROWS = D * ROW_ADA + ROW_BIAS
BASE_FINAL = BASE_LAYER + LAYERS * LAYER_ROWS
ROW_FINAL = 2 * ROW_D
BASE_TAIL = BASE_FINAL + D * ROW_FINAL
ROW_TAIL = ROW_FINAL + PATCH * ROW_D
FRONT = 56


def time_freq(step):
    half = FREQ // 2
    freqs = jnp.exp(-math.log(10000.0) * jnp.arange(half).astype(F32) / half)
    angles = step.astype(F32) * freqs
    return jnp.concatenate([jnp.cos(angles), jnp.sin(angles)])


def place_embed(slots, width):
    quarter = D // 4
    omega = jnp.power(10000.0, -jnp.arange(quarter).astype(F32) / quarter)
    row_angle = (slots // width).astype(F32)[:, None] * omega
    col_angle = (slots % width).astype(F32)[:, None] * omega
    return jnp.concatenate(
        [jnp.sin(row_angle), jnp.cos(row_angle), jnp.sin(col_angle), jnp.cos(col_angle)], axis=1
    )


def normalize(state):
    centered = state - jnp.mean(state, axis=-1, keepdims=True)
    spread = jnp.mean(centered * centered, axis=-1, keepdims=True)
    return centered * lax.rsqrt(spread + NORM_EPS)


def modulate(state, shift, scale):
    return normalize(state) * (1.0 + scale) + shift


def gelu_tanh(value):
    return jax.nn.gelu(value, approximate=True)


def contract_rows(left, right):
    return lax.dot_general(left, right, (((0,), (0,)), ((), ())), preferred_element_type=F32)


def contract_cols(left, right):
    return lax.dot_general(left, right, (((1,), (1,)), ((), ())), preferred_element_type=F32)


def bits_of(axis):
    size = lax.axis_size(axis)
    return [1 << k for k in range(size.bit_length() - 1)]


def swap_by(value, axis, bit):
    size = lax.axis_size(axis)
    return lax.ppermute(value, axis, [(i, i ^ bit) for i in range(size)])


def all_sum(value, axes=("c", "x", "y", "z")):
    for axis in axes:
        for bit in bits_of(axis):
            value = value + swap_by(value, axis, bit)
    return value


def gather_rows(value, axes):
    for axis in axes:
        for bit in bits_of(axis):
            other = swap_by(value, axis, bit)
            low = (lax.axis_index(axis) & bit) == 0
            value = jnp.where(
                low, jnp.concatenate([value, other]), jnp.concatenate([other, value])
            )
    return value


def scatter_rows(value, axes):
    for axis in axes:
        for bit in reversed(bits_of(axis)):
            halves = value.reshape((2, value.shape[0] // 2) + value.shape[1:])
            side = jnp.where((lax.axis_index(axis) & bit) == 0, 0, 1)
            send = lax.dynamic_index_in_dim(halves, 1 - side, 0, keepdims=False)
            keep = lax.dynamic_index_in_dim(halves, side, 0, keepdims=False)
            value = keep + swap_by(send, axis, bit)
    return value


def own_sequence(values):
    x = lax.axis_index("x")
    send = lax.dynamic_index_in_dim(values, 1 - x, 0, keepdims=False)
    keep = lax.dynamic_index_in_dim(values, x, 0, keepdims=False)
    other = lax.ppermute(send, "x", SWAP)
    pair = jnp.where(x == 0, jnp.stack([keep, other]), jnp.stack([other, keep]))
    more = lax.ppermute(pair, "c", SWAP)
    both = jnp.where(
        lax.axis_index("c") == 0, jnp.stack([pair, more], 1), jnp.stack([more, pair], 1)
    )
    return both.transpose(2, 0, 1, 3).reshape(values.shape[1], -1)


def strips_of(tiles, is_mixer):
    count = tiles.shape[0] // 12
    plain = (
        tiles.reshape(count, 3, 4, BLK, BLK).transpose(0, 1, 3, 2, 4).reshape(count, STRIP, D)
    )
    turned = (
        tiles.reshape(count, 4, 3, BLK, BLK).transpose(0, 2, 4, 1, 3).reshape(count, STRIP, D)
    )
    return jnp.where(is_mixer, turned, plain)


def tiles_of(strips, is_mixer):
    count = strips.shape[0]
    plain = (
        strips.reshape(count, 3, BLK, 4, BLK).transpose(0, 1, 3, 2, 4).reshape(-1, BLK, BLK)
    )
    turned = (
        strips.reshape(count, 3, BLK, 4, BLK).transpose(0, 3, 1, 4, 2).reshape(-1, BLK, BLK)
    )
    return jnp.where(is_mixer, turned, plain)


def select_y(own, other):
    first = lax.axis_index("y") == 0
    return jnp.where(first, own, other), jnp.where(first, other, own)


HALF = STRIP // 2


def gather_strips(strip):
    z = lax.axis_index("z")
    halves = []
    for part in (strip[:HALF], strip[HALF:]):
        right, left = [part], [part]
        for hop in range(3):
            right.append(lax.ppermute(right[-1], "z", [(i, i + 1) for i in range(hop, 3)]))
            left.append(lax.ppermute(left[-1], "z", [(i + 1, i) for i in range(3 - hop)]))
        halves.append((right, left))
    planes = []
    for plane in range(4):
        columns = []
        for right, left in halves:
            column = right[0]
            for place in range(4):
                if place > plane:
                    column = jnp.where(z == place, right[place - plane], column)
                elif place < plane:
                    column = jnp.where(z == place, left[plane - place], column)
            columns.append(column)
        upper, lower = columns
        upper_x = lax.ppermute(upper, "x", SWAP)
        upper_y = lax.ppermute(jnp.stack([upper, upper_x]), "y", SWAP)
        lower_y = lax.ppermute(lower, "y", SWAP)
        lower_x = lax.ppermute(jnp.stack([lower, lower_y]), "x", SWAP)
        own_y = [
            jnp.concatenate([upper, lower]),
            jnp.concatenate([upper_x, lower_x[0]]),
        ]
        other_y = [
            jnp.concatenate([upper_y[0], lower_y]),
            jnp.concatenate([upper_y[1], lower_x[1]]),
        ]
        planes.append([select_y(own_y[i], other_y[i]) for i in range(2)])
    return planes


def gather_any(tiles):
    whole = lax.all_gather(tiles, ("z", "y", "x"), axis=0, tiled=False)
    x = lax.axis_index("x")
    whole = whole.reshape((-1, 2) + tiles.shape)
    groups = []
    for place in (x, 1 - x):
        blocks = lax.dynamic_index_in_dim(whole, place, 1, keepdims=False)
        blocks = blocks.reshape(-1, BLK, BLK)
        groups.append(strips_of(blocks, (jnp.arange(8) % 4 == 0)[:, None, None]))
    return [
        [(groups[i][2 * plane], groups[i][2 * plane + 1]) for i in range(2)] for plane in range(4)
    ]


def add_low(left, right):
    return (left.astype(F32) + right.astype(F32)).astype(BF16)


def reduce_plane(grads):
    y = lax.axis_index("y")

    def pick(pair, own):
        first = (y == 0) if own else (y == 1)
        return jnp.where(first, pair[0], pair[1])

    own_x = [part[:HALF] for part in grads[0]]
    send_x = jnp.stack([part[:HALF] for part in grads[1]])
    got = lax.ppermute(send_x, "x", SWAP)
    upper = [add_low(own_x[i], got[i]) for i in range(2)]
    got = lax.ppermute(pick(upper, False), "y", SWAP)
    upper = add_low(pick(upper, True), got)
    lows = [[part[HALF:] for part in group] for group in grads]
    got = lax.ppermute(jnp.stack([pick(group, False) for group in lows]), "y", SWAP)
    lower = [add_low(pick(lows[i], True), got[i]) for i in range(2)]
    got = lax.ppermute(lower[1], "x", SWAP)
    lower = add_low(lower[0], got)
    return [upper, lower]


def reduce_line(part, plane):
    rights, lefts = plane, 3 - plane
    hops = max(rights, lefts)
    for hop in range(hops):
        pairs = []
        if hop < rights:
            pairs.append((hop, hop + 1))
        if hop < lefts:
            pairs.append((3 - hop, 2 - hop))
        if len(pairs) == 2 and pairs[0][1] == pairs[1][1]:
            one = lax.ppermute(part, "z", [pairs[0]])
            two = lax.ppermute(part, "z", [pairs[1]])
            part = add_low(part, one.astype(F32) + two.astype(F32))
        else:
            part = add_low(part, lax.ppermute(part, "z", pairs))
    return part


def reduce_any(planes, count):
    x = lax.axis_index("x")
    groups = []
    for place in range(2):
        chosen = [
            jnp.where(x == place, planes[plane][0][y], planes[plane][1][y])
            for plane in range(4)
            for y in range(2)
        ]
        blocks = tiles_of(jnp.stack(chosen), jnp.zeros((), bool)).reshape(8, 12, BLK, BLK)
        turned = tiles_of(jnp.stack(chosen), jnp.ones((), bool)).reshape(8, 12, BLK, BLK)
        mixer = (jnp.arange(8) % 4 == 0)[:, None, None, None]
        groups.append(jnp.where(mixer, turned, blocks).reshape(-1, count, BLK, BLK))
    whole = jnp.stack(groups, axis=1).reshape(-1, BLK, BLK)
    return lax.psum_scatter(whole, ("z", "y", "x"), scatter_dimension=0, tiled=True)


class Flat:
    def __init__(self, length):
        size = lax.axis_size("z") * lax.axis_size("y") * lax.axis_size("x") * lax.axis_size("c")
        del size
        index = lax.axis_index("z")
        for axis in ("y", "x", "c"):
            index = index * lax.axis_size(axis) + lax.axis_index(axis)
        start = index * length
        self.length = length
        self.first = start // LANE
        self.skew = start % LANE
        self.rows = -(-(length + LANE - 1) // LANE)
        self.back = self.rows + 2 * ROW_ADA
        self.total = -(-(FRONT + self.rows + self.back) // 8) * 8

    def align(self, shard):
        empty = jnp.zeros((self.total * LANE,), shard.dtype)
        return lax.dynamic_update_slice(empty, shard, (FRONT * LANE + self.skew,)).reshape(
            self.total, LANE
        )

    def unalign(self, rows):
        return lax.dynamic_slice(
            rows.reshape(-1), (FRONT * LANE + self.skew,), (self.length,)
        )

    def place(self, base, width, height):
        count = min(height, self.rows // width + 2)
        skip = jnp.clip((self.first - base) // width, 0, height)
        at = jnp.minimum(base + skip * width - self.first, self.rows) + FRONT
        return count, skip, at

    def part(self, rows, base, width, height):
        count, skip, at = self.place(base, width, height)
        piece = lax.dynamic_slice(rows, (at, 0), (count * width, LANE))
        return piece.reshape(count, width * LANE), count, skip

    def product(self, rows, factor, base, width, precision=None):
        height = factor.shape[1]
        piece, count, skip = self.part(rows, base, width, height)
        padded = jnp.pad(factor, ((0, 0), (0, count)))
        near = lax.dynamic_slice(padded, (0, skip), (factor.shape[0], count))
        return jnp.dot(near, piece, precision=precision, preferred_element_type=F32)

    def back_product(self, rows, grad, base, width, height):
        piece, count, skip = self.part(rows, base, width, height)
        piece = piece.astype(F32)
        near = lax.dot_general(
            grad, piece, (((1,), (1,)), ((), ())), precision=HIGH, preferred_element_type=F32
        )
        empty = jnp.zeros((grad.shape[0], height + count), F32)
        return lax.dynamic_update_slice(empty, near, (0, skip))[:, :height]

    def take(self, rows, base, height):
        count, skip, at = self.place(base, 1, height)
        count = height
        piece = lax.dynamic_slice(rows, (at, 0), (count, LANE))
        keep = jnp.arange(count) < height - skip
        piece = jnp.where(keep[:, None], piece, 0)
        empty = jnp.zeros((2 * height, LANE), rows.dtype)
        return lax.dynamic_update_slice(empty, piece, (skip, 0))[:height]

    def put_outer(self, rows, left, right, base, width):
        height = left.shape[1]
        count, skip, at = self.place(base, width, height)
        padded = jnp.pad(left, ((0, 0), (0, count)))
        near = lax.dynamic_slice(padded, (0, skip), (left.shape[0], count))
        piece = lax.dot_general(
            near, right, (((0,), (0,)), ((), ())), precision=HIGH, preferred_element_type=F32
        )
        return lax.dynamic_update_slice(rows, piece.reshape(count * width, LANE), (at, 0))

    def put_rows(self, rows, vector, base):
        height = vector.shape[0]
        unused, skip, at = self.place(base, 1, height)
        padded = jnp.pad(vector, ((0, height), (0, 0)))
        near = lax.dynamic_slice(padded, (skip, 0), (height, LANE))
        return lax.dynamic_update_slice(rows, near, (at, 0))


def split_heads(mixed):
    rows = mixed.shape[0]
    heads = mixed.shape[1] // (3 * HD)
    shaped = mixed.reshape(rows, 3, heads, HD)
    return (shaped[:, 0], shaped[:, 1], shaped[:, 2])


def query_block(rows):
    return 512 if rows % 512 == 0 else rows


def attend_forward(mixed, keymask):
    query, keys, values = split_heads(mixed)
    rows, heads = (query.shape[0], query.shape[1])
    block = query_block(rows)
    scale = HD ** (-0.5)

    def one_block(block_query):
        raw = (
            jnp.einsum("qhd,khd->hqk", block_query, keys, preferred_element_type=F32)
            * scale
        )
        scores = jnp.where(keymask[None, None, :], raw, -1e30)
        top = jnp.max(scores, axis=-1, keepdims=True)
        expo = jnp.exp(scores - top)
        total = jnp.sum(expo, axis=-1, keepdims=True)
        probs = (expo / total).astype(BF16)
        out = jnp.einsum("hqk,khd->qhd", probs, values, preferred_element_type=F32)
        return (out, (top + jnp.log(total))[..., 0])

    outs, log_total = lax.map(one_block, query.reshape(rows // block, block, heads, HD))
    return (outs.reshape(rows, heads * HD).astype(BF16), log_total)


def attend_backward(mixed, keymask, log_total, attended, grad_out):
    query, keys, values = split_heads(mixed)
    rows, heads = (query.shape[0], query.shape[1])
    block = query_block(rows)
    scale = HD ** (-0.5)

    def one_block(carry, inputs):
        grad_keys, grad_values = carry
        block_query, block_total, block_grad = inputs
        raw = (
            jnp.einsum("qhd,khd->hqk", block_query, keys, preferred_element_type=F32)
            * scale
        )
        scores = jnp.where(keymask[None, None, :], raw, -1e30)
        probs = jnp.exp(scores - block_total[..., None])
        grad_probs = jnp.einsum("qhd,khd->hqk", block_grad, values, preferred_element_type=F32)
        delta = jnp.sum(grad_probs * probs, axis=-1, keepdims=True)
        grad_scores = (probs * (grad_probs - delta)).astype(BF16)
        grad_query = (
            jnp.einsum("hqk,khd->qhd", grad_scores, keys, preferred_element_type=F32)
            * scale
        )
        grad_keys = (
            grad_keys
            + jnp.einsum("hqk,qhd->khd", grad_scores, block_query, preferred_element_type=F32)
            * scale
        )
        grad_values = grad_values + jnp.einsum(
            "hqk,qhd->khd", probs.astype(BF16), block_grad, preferred_element_type=F32
        )
        return ((grad_keys, grad_values), grad_query)

    empty = jnp.zeros(keys.shape, F32)
    shaped = (
        query.reshape(rows // block, block, heads, HD),
        log_total,
        grad_out.reshape(rows // block, block, heads, HD),
    )
    (grad_keys, grad_values), grad_query = lax.scan(one_block, (empty, empty), shaped)
    return (
        jnp.stack([grad_query.reshape(rows, heads, HD), grad_keys, grad_values], axis=1)
        .reshape(mixed.shape)
        .astype(BF16)
    )


def join_cores(partial):
    low = partial.astype(BF16)
    return low.astype(F32) + lax.ppermute(low, "c", SWAP).astype(F32)


def rank_columns(vector, groups, rank, ranks):
    return lax.dynamic_index_in_dim(
        vector.reshape(groups, ranks, -1), rank, 1, keepdims=False
    ).reshape(-1)


def spread_columns(grads, groups, ranks_here, ranks):
    total = 0.0
    for grad, rank in zip(grads, ranks_here):
        width = grad.shape[0] // groups
        select = (jnp.arange(ranks) == rank).astype(F32)
        total = total + (grad.reshape(groups, 1, width) * select[None, :, None]).reshape(-1)
    return total


def layer_forward(state, modulation, biases, mats, keymask, ranks_here, ranks):
    qkv_b, proj_b, up_b, down_b = biases
    shift_a, scale_a, gate_a, shift_b, scale_b, gate_b = jnp.split(modulation, 6)
    normed_a = modulate(state, shift_a, scale_a).astype(BF16)
    mixed, log_total, attended = ([], [], [])
    partial = 0.0
    for mat, rank in zip(mats, ranks_here):
        bias = rank_columns(qkv_b, 3, rank, ranks)
        one = (contract_cols(normed_a, mat[0]) + bias).astype(BF16)
        out, total = attend_forward(one, keymask)
        mixed.append(one)
        log_total.append(total)
        attended.append(out)
        partial = partial + jnp.dot(out, mat[1], preferred_element_type=F32)
    attn = join_cores(partial) + proj_b
    middle = state + gate_a * attn
    normed_b = modulate(middle, shift_b, scale_b).astype(BF16)
    pre_act, active = ([], [])
    partial = 0.0
    for mat, rank in zip(mats, ranks_here):
        bias = rank_columns(up_b, 1, rank, ranks)
        pre = jnp.dot(normed_b, mat[2], preferred_element_type=F32) + bias
        act = gelu_tanh(pre).astype(BF16)
        pre_act.append(pre)
        active.append(act)
        partial = partial + jnp.dot(act, mat[3], preferred_element_type=F32)
    mlp = join_cores(partial) + down_b
    kept = (state, normed_a, mixed, log_total, attended, attn, middle, normed_b, pre_act, active, mlp)
    return (middle + gate_b * mlp, kept)


def layer_backward(grad_out, modulation, mats, kept, keymask, ranks_here, ranks):
    state, normed_a, mixed, log_total, attended, attn, middle, normed_b, pre_act, active, mlp = kept
    shift_a, scale_a, gate_a, shift_b, scale_b, gate_b = jnp.split(modulation, 6)
    grad_gate_b = jnp.sum(grad_out * mlp, axis=0)
    grad_mlp = gate_b * grad_out
    grad_down_b = jnp.sum(grad_mlp, axis=0)
    grad_mlp = grad_mlp.astype(BF16)
    grad_up, grad_down, grad_up_b = ([], [], [])
    partial = 0.0
    for mat, pre, act in zip(mats, pre_act, active):
        grad_down.append(contract_rows(act, grad_mlp).astype(BF16))
        grad_act = contract_cols(grad_mlp, mat[3])
        unused, gelu_pull = jax.vjp(gelu_tanh, pre)
        grad_pre = gelu_pull(grad_act)[0].astype(BF16)
        grad_up_b.append(jnp.sum(grad_pre.astype(F32), axis=0))
        grad_up.append(contract_rows(normed_b, grad_pre).astype(BF16))
        partial = partial + contract_cols(grad_pre, mat[2])
    unused, pull_b = jax.vjp(modulate, middle, shift_b, scale_b)
    grad_inner, grad_shift_b, grad_scale_b = pull_b(join_cores(partial))
    grad_middle = grad_out + grad_inner
    grad_gate_a = jnp.sum(grad_middle * attn, axis=0)
    grad_attn = gate_a * grad_middle
    grad_proj_b = jnp.sum(grad_attn, axis=0)
    grad_attn = grad_attn.astype(BF16)
    grad_proj, grad_mixer, grad_qkv_b = ([], [], [])
    partial = 0.0
    for mat, one, total, out in zip(mats, mixed, log_total, attended):
        grad_proj.append(contract_rows(out, grad_attn).astype(BF16))
        grad_attended = contract_cols(grad_attn, mat[1]).astype(BF16)
        grad_mixed = attend_backward(one, keymask, total, out, grad_attended)
        grad_qkv_b.append(jnp.sum(grad_mixed.astype(F32), axis=0))
        grad_mixer.append(contract_rows(grad_mixed, normed_a).astype(BF16))
        partial = partial + jnp.dot(grad_mixed, mat[0], preferred_element_type=F32)
    unused, pull_a = jax.vjp(modulate, state, shift_a, scale_a)
    grad_state, grad_shift_a, grad_scale_a = pull_a(join_cores(partial))
    grad_mod = jnp.concatenate(
        [grad_shift_a, grad_scale_a, grad_gate_a, grad_shift_b, grad_scale_b, grad_gate_b]
    )
    once = jnp.where(lax.axis_index("c") == 0, 1.0, 0.0)
    grad_bias = jnp.concatenate(
        [
            spread_columns(grad_qkv_b, 3, ranks_here, ranks),
            grad_proj_b * once,
            spread_columns(grad_up_b, 1, ranks_here, ranks),
            grad_down_b * once,
        ]
    )
    split = 2 * BLK
    upper = [
        (grad_mixer[i], jnp.concatenate([grad_proj[i], grad_up[i][:split]])) for i in range(2)
    ]
    lower = [
        (jnp.concatenate([grad_up[i][split:], grad_down[i][:BLK]]), grad_down[i][BLK:])
        for i in range(2)
    ]
    return (grad_middle + grad_state, grad_mod, grad_bias, [upper, lower])


def adamw(grad, moment, second, master):
    new_moment = ADAM_ONE * moment + (1.0 - ADAM_ONE) * grad
    new_second = ADAM_TWO * second + (1.0 - ADAM_TWO) * grad * grad
    fixed_moment = new_moment / (1.0 - ADAM_ONE**STEP_COUNT)
    fixed_second = new_second / (1.0 - ADAM_TWO**STEP_COUNT)
    new_master = master - ADAM_RATE * (
        fixed_moment / (jnp.sqrt(fixed_second) + ADAM_EPS) + ADAM_DECAY * master
    )
    return (new_moment, new_second, new_master)


def shampoo(grad, moment, left, right, left_inv, right_inv, master):
    new_left = SHAMPOO_TWO * left + (1.0 - SHAMPOO_TWO) * jnp.einsum(
        "tij,tkj->tik", grad, grad, precision=HIGH
    )
    new_right = SHAMPOO_TWO * right + (1.0 - SHAMPOO_TWO) * jnp.einsum(
        "tji,tjk->tik", grad, grad, precision=HIGH
    )
    new_moment = SHAMPOO_ONE * moment + (1.0 - SHAMPOO_ONE) * grad
    halfway = jnp.einsum("tij,tjk->tik", left_inv, new_moment, precision=HIGH)
    direction = jnp.einsum("tij,tjk->tik", halfway, right_inv, precision=HIGH)
    new_master = master - SHAMPOO_RATE * (direction + SHAMPOO_DECAY * master)
    return (new_moment, new_left, new_right, new_master)


def local(
    latents,
    noise,
    timesteps,
    labels,
    grid,
    flat_master,
    flat_moment,
    flat_second,
    tile_master,
    tile_moment,
    tile_left,
    tile_right,
    left_root,
    right_root,
):
    x, y, z, c = [lax.axis_index(name) for name in ("x", "y", "z", "c")]
    groups = lax.axis_size("z") * lax.axis_size("y")
    ranks = lax.axis_size("x") * lax.axis_size("c")
    count_tiles = tile_master.shape[1]
    simple = lax.axis_size("y") == 2 and lax.axis_size("z") == 4 and count_tiles == 12
    ranks_here = [2 * x + c, 2 * (1 - x) + c]
    number = (z * lax.axis_size("y") + y) * 2 + x

    owner = z * lax.axis_size("y") + y
    if simple:
        is_mixer = owner % 4 == 0
        strip = strips_of(tile_master[0].astype(BF16), is_mixer)[0]
        planes = gather_strips(strip)
    else:
        planes = gather_any(tile_master[0].astype(BF16))
    mats = []
    for layer in range(LAYERS):
        per_rank = []
        for i in range(2):
            (mixer, mid), (low, last) = planes[2 * layer][i], planes[2 * layer + 1][i]
            per_rank.append(
                (
                    mixer,
                    mid[:BLK],
                    jnp.concatenate([mid[BLK:], low[: 2 * BLK]]),
                    jnp.concatenate([low[2 * BLK :], last]),
                )
            )
        mats.append(per_rank)

    info = jnp.concatenate(
        [timesteps[:, 0], labels[:, 0], grid[:, 0, 0], grid[:, 1, 0]]
    ).reshape(1, 4, MB)
    info = gather_rows(info, ("y", "z"))
    info = info.transpose(1, 0, 2).reshape(4, groups * MB)
    count = jnp.sum((info[2] * info[3]).astype(F32))
    height = lax.dynamic_index_in_dim(info[2], number, 0, keepdims=False)
    width = lax.dynamic_index_in_dim(info[3], number, 0, keepdims=False)
    patches = own_sequence(latents)
    target = own_sequence(noise)
    rows = patches.shape[1]
    slots = jnp.arange(rows)
    valid = slots < height * width

    flat = Flat(flat_master.shape[0])
    held = flat.align(flat_master.astype(BF16))
    held_f32 = held.astype(F32)
    small = jnp.concatenate(
        [flat.take(held_f32, 0, ROW_STEM)]
        + [flat.take(held_f32, BASE_B1, ROW_D), flat.take(held_f32, BASE_B2, ROW_D)]
        + [
            flat.take(held_f32, BASE_LAYER + l * LAYER_ROWS + D * ROW_ADA, ROW_BIAS)
            for l in range(LAYERS)
        ]
        + [flat.take(held_f32, BASE_TAIL, ROW_TAIL)]
    )
    small = all_sum(small.astype(BF16)).astype(F32)
    pieces = []
    at = 0
    for amount in [ROW_STEM, ROW_D, ROW_D] + [ROW_BIAS] * LAYERS + [ROW_TAIL]:
        pieces.append(small[at : at + amount].reshape(-1))
        at = at + amount
    stem, time_b1, time_b2 = pieces[:3]
    tail = pieces[-1]
    patch_w, patch_b = stem[: PATCH * D].reshape(PATCH, D), stem[PATCH * D :]
    final_b, head_w = tail[: 2 * D], tail[2 * D :].reshape(D, PATCH).astype(BF16)
    biases, ada_bs = ([], [])
    for layer in range(LAYERS):
        vector = pieces[3 + layer]
        ada_bs.append(vector[: 6 * D])
        biases.append(jnp.split(vector[6 * D :], [3 * D, 4 * D, 8 * D]))

    freq = jax.vmap(time_freq)(info[0])
    onehot = (jnp.arange(CLASSES)[None, :] == info[1][:, None]).astype(F32)
    hidden_pre = (
        all_sum(flat.product(held_f32, freq, BASE_W1, ROW_D, HIGH)) + time_b1
    )
    hidden = jax.nn.silu(hidden_pre)
    cond = flat.product(held_f32, hidden, BASE_W2, ROW_D, HIGH)
    cond = cond + flat.product(held_f32, onehot, BASE_TABLE, ROW_D)
    cond = all_sum(cond) + time_b2
    cond_s = jax.nn.silu(cond).astype(BF16)
    mods = jnp.concatenate(
        [
            flat.product(held, cond_s, BASE_LAYER + l * LAYER_ROWS, ROW_ADA)
            for l in range(LAYERS)
        ]
        + [flat.product(held, cond_s, BASE_FINAL, ROW_FINAL)],
        axis=1,
    )
    mods = all_sum(scatter_rows(mods, ("z", "y", "x")), ("c",))[0]
    modulations = [mods[l * 6 * D : (l + 1) * 6 * D] + ada_bs[l] for l in range(LAYERS)]
    final_mod = mods[LAYERS * 6 * D :] + final_b

    state = contract_rows(patches, patch_w.astype(BF16)) + patch_b + place_embed(slots, width)
    kept = [None] * LAYERS
    for layer in range(LAYERS):
        state, kept[layer] = layer_forward(
            state, modulations[layer], biases[layer], mats[layer], valid, ranks_here, ranks
        )
    shift_f, scale_f = jnp.split(final_mod, 2)
    normed_f = modulate(state, shift_f, scale_f).astype(BF16)
    predicted = jnp.dot(normed_f, head_w, preferred_element_type=F32)
    error = predicted - target.T
    loss_part = jnp.sum(jnp.where(valid[:, None], error * error, 0.0))
    grad_pred = jnp.where(valid[:, None], 2.0 * error / (PATCH * count), 0.0).astype(BF16)

    grad_head = contract_rows(normed_f, grad_pred)
    grad_normed_f = contract_cols(grad_pred, head_w)
    unused, pull_f = jax.vjp(modulate, state, shift_f, scale_f)
    grad_state, grad_shift_f, grad_scale_f = pull_f(grad_normed_f)
    grad_final = jnp.concatenate([grad_shift_f, grad_scale_f])
    grad_mods, grad_biases = ([None] * LAYERS, [None] * LAYERS)
    grad_planes = [None] * 4
    for layer in reversed(range(LAYERS)):
        grad_state, grad_mods[layer], grad_biases[layer], both = layer_backward(
            grad_state, modulations[layer], mats[layer], kept[layer], valid, ranks_here, ranks
        )
        grad_planes[2 * layer], grad_planes[2 * layer + 1] = both
    if simple:
        mine = None
        for plane in reversed(range(4)):
            halves = [reduce_line(part, plane) for part in reduce_plane(grad_planes[plane])]
            whole = jnp.concatenate(halves)
            mine = whole if mine is None else jnp.where(z == plane, whole, mine)
        grad_tiles = tiles_of(mine[None], is_mixer).astype(F32)
    else:
        grad_tiles = reduce_any(grad_planes, count_tiles).astype(F32)
    grad_patch_b = jnp.sum(grad_state, axis=0)
    grad_patch_w = jnp.dot(patches.astype(F32), grad_state, precision=HIGH)
    once = jnp.where(c == 0, 1.0, 0.0)
    summed = jnp.concatenate(
        [grad_patch_w.reshape(-1) * once, grad_patch_b * once]
        + grad_biases
        + [grad_head.reshape(-1) * once, jnp.pad(loss_part[None] * once, (0, LANE - 1))]
    )
    summed = all_sum(summed.reshape(-1, LANE))
    stem_rows = summed[:ROW_STEM]
    extra = ROW_BIAS - ROW_ADA
    bias_rows = [summed[ROW_STEM + l * extra : ROW_STEM + (l + 1) * extra] for l in range(LAYERS)]
    head_rows = summed[ROW_STEM + LAYERS * extra : -1]
    summed_loss = summed[-1, 0]

    all_mods = gather_rows(
        jnp.concatenate(grad_mods + [grad_final])[None], ("x", "y", "z")
    )
    mods_of = [all_mods[:, l * 6 * D : (l + 1) * 6 * D] for l in range(LAYERS)]
    final_of = all_mods[:, LAYERS * 6 * D :]
    grad_cond = flat.back_product(held, final_of, BASE_FINAL, ROW_FINAL, D)
    for layer in range(LAYERS):
        grad_cond = grad_cond + flat.back_product(
            held, mods_of[layer], BASE_LAYER + layer * LAYER_ROWS, ROW_ADA, D
        )
    grad_cond = all_sum(grad_cond)
    grad_cond = jax.vjp(jax.nn.silu, cond)[1](grad_cond)[0]
    grad_hidden = all_sum(flat.back_product(held, grad_cond, BASE_W2, ROW_D, D))
    grad_hidden = jax.vjp(jax.nn.silu, hidden_pre)[1](grad_hidden)[0]

    def total_rows(values):
        return jnp.sum(values, axis=0).reshape(-1, LANE)

    cond_f = cond_s.astype(F32)
    out = jnp.zeros((flat.total, LANE), F32)
    out = flat.put_rows(out, stem_rows, 0)
    out = flat.put_outer(out, freq, grad_hidden, BASE_W1, ROW_D)
    out = flat.put_rows(out, total_rows(grad_hidden), BASE_B1)
    out = flat.put_outer(out, hidden, grad_cond, BASE_W2, ROW_D)
    out = flat.put_rows(out, total_rows(grad_cond), BASE_B2)
    out = flat.put_outer(out, onehot, grad_cond, BASE_TABLE, ROW_D)
    for layer in range(LAYERS):
        base = BASE_LAYER + layer * LAYER_ROWS
        out = flat.put_outer(out, cond_f, mods_of[layer], base, ROW_ADA)
        vector = jnp.concatenate([total_rows(mods_of[layer]), bias_rows[layer]])
        out = flat.put_rows(out, vector, base + D * ROW_ADA)
    out = flat.put_outer(out, cond_f, final_of, BASE_FINAL, ROW_FINAL)
    out = flat.put_rows(out, jnp.concatenate([total_rows(final_of), head_rows]), BASE_TAIL)
    grad_flat = flat.unalign(out)

    square = jnp.sum(grad_flat * grad_flat) + jnp.sum(grad_tiles * grad_tiles)
    norm = jnp.sqrt(all_sum(square.reshape(1, 1))[0, 0])
    factor = jnp.minimum(1.0, CLIP_AT / (norm + 1e-06))
    new_moment, new_second, new_flat = adamw(
        grad_flat * factor, flat_moment, flat_second, flat_master
    )
    tile_mom, new_left, new_right, new_tiles = shampoo(
        grad_tiles * factor,
        tile_moment[0],
        tile_left[0],
        tile_right[0],
        left_root[0],
        right_root[0],
        tile_master[0],
    )
    return (
        summed_loss,
        count,
        norm,
        new_moment,
        new_second,
        new_flat,
        tile_mom[None],
        new_left[None],
        new_right[None],
        new_tiles[None],
    )


def solution(mesh):
    deep = 4
    axes = Mesh(
        mesh.devices.reshape(deep, mesh.shape["dp"] // deep, MB, mesh.shape["mp"] // MB),
        ("z", "y", "x", "c"),
    )
    dp, mp, whole = ("z", "y"), ("x", "c"), ("z", "y", "x", "c")
    tile = P(mp, dp, None, None)
    in_specs = (
        P(None, None, whole),
        P(None, None, whole),
        P(None, dp),
        P(None, dp),
        P(None, None, dp),
        P(whole),
        P(whole),
        P(whole),
    ) + (tile,) * 6
    out_specs = (P(), P(), P(), P(whole), P(whole), P(whole)) + (tile,) * 4
    return jax.shard_map(local, mesh=axes, in_specs=in_specs, out_specs=out_specs, check_vma=False)
```

profile of v0, /device:TPU:0, one launch (start us, length us, event | category | flops | bytes accessed | tf_op | source)
XLA Modules:
  0.0 1893.8 jit_solution(12674502733973219094)
XLA Ops:
  19.4 5.9 collective-permute-start.25
  26.5 5.9 collective-permute-start.28
  37.5 20.8 %dynamic_update_slice.107 = bf16[1360896]{0:T(1024)(128)(2,1)S(1)} dynamic-update-slice(bf16[1360896]{0:T(1024)(128)(2,1)S(1)} %broadcast_in_dim.334, bf16[669708]{0:T(1024)(128)(2,1)} %convert_element_type.927, s32[]{:T(128)S(6)} %select_n.764) | dynamic-update-slice | bytes 2678836 | tf_op jit(solution)/shard_map/dynamic_update_slice | solution.py:307
  136.8 14.1 multiply_cosine_fusion
  153.0 6.6 concatenate.217
  174.0 22.1 %collective-permute-done.18 = f32[16,1152]{1,0:T(8,128)} collective-permute-done((f32[16,1152]{1,0:T(8,128)S(1)}, f32[16,1152]{1,0:T(8,128)}, u32[]{:S(2)}, u32[]{:S(2)}) %collective-permute-start.18) | collective-permute-done | bytes 73760 | tf_op jit(solution)/shard_map/ppermute | solution.py:104
  209.8 16.6 collective-permute-done.20
  246.5 17.5 collective-permute-done.43
  271.8 13.6 collective-permute-done.44
  287.8 18.9 collective-permute-done.50
  312.6 13.2 collective-permute-done.51
  332.6 24.3 %collective-permute-done.31 = bf16[432,1152]{1,0:T(8,128)(2,1)S(1)} collective-permute-done((bf16[432,1152]{1,0:T(8,128)(2,1)S(1)}, bf16[432,1152]{1,0:T(8,128)(2,1)S(1)}, u32[]{:S(2)}, u32[]{:S(2)}) %collective-permute-start.31) | collective-permute-done | bytes 995360 | tf_op jit(solution)/shard_map/ppermute | solution.py:200
  366.3 11.8 collective-permute-done.38
  381.4 43.3 %collective-permute-done.40 = bf16[432,1152]{1,0:T(8,128)(2,1)S(1)} collective-permute-done((bf16[432,1152]{1,0:T(8,128)(2,1)S(1)}, bf16[432,1152]{1,0:T(8,128)(2,1)S(1)}, u32[]{:S(2)}, u32[]{:S(2)}) %collective-permute-start.40) | collective-permute-done | bytes 995360 | tf_op jit(solution)/shard_map/ppermute | solution.py:202
  436.0 14.1 while.112
  450.1 18.1 collective-permute-done.34
  474.1 12.5 while.113
  566.0 12.7 while.114
  585.1 12.5 while.115
  635.1 5.8 add_convert_fusion.5
  661.0 6.0 multiply_reduce_fusion.6
  667.0 7.8 convert_reduce_fusion
  674.9 8.2 convert_reduce_fusion.1
  745.1 57.6 %while.117 = (s32[]{:T(128)}, f32[1024,4,72]{0,2,1:T(8,128)S(1)}, f32[1024,4,72]{0,2,1:T(8,128)}, bf16[2,512,4,72]{1,0,3,2:T(2,128)(2,1)}, bf16[2,512,4,72]{1,3,...) while((s32[]{:T(128)}, f32[1024,4,72]{0,2,1:T(8,128)S(1)}, ...), condition=%wide.region_36.37_spmd.clone, body=%wide.region_34.36_spmd.clone.sunk | while | flops 1543175168 | bytes 160788816 | solution.py:442
  753.9 11.8 dynamic_update_slice.171
  782.2 11.8 dynamic_update_slice.171
  822.3 57.6 %while.116 = (s32[]{:T(128)}, f32[1024,4,72]{0,2,1:T(8,128)S(1)}, f32[1024,4,72]{0,2,1:T(8,128)}, bf16[2,512,4,72]{1,0,3,2:T(2,128)(2,1)}, bf16[2,512,4,72]{1,3,...) while((s32[]{:T(128)}, f32[1024,4,72]{0,2,1:T(8,128)S(1)}, ...), condition=%wide.region_33.34_spmd.clone, body=%wide.region_31.33_spmd.clone.sunk | while | flops 1543175168 | bytes 160788816 | solution.py:442
  831.2 11.8 dynamic_update_slice.170
  859.4 11.8 dynamic_update_slice.170
  903.9 6.0 broadcast_select_fusion.16
  932.1 7.8 convert_reduce_fusion.2
  940.0 8.0 convert_reduce_fusion.3
  978.0 63.8 %collective-permute-done.101 = bf16[432,1152]{1,0:T(8,128)(2,1)} collective-permute-done((bf16[432,1152]{1,0:T(8,128)(2,1)}, bf16[432,1152]{1,0:T(8,128)(2,1)}, u32[]{:S(2)}, u32[]{:S(2)}) %collective-permute-start.101) | collective-permute-done | bytes 995360 | tf_op jit(solution)/shard_map/ppermute | solution.py:245
  1053.7 12.5 collective-permute-done.102
  1091.1 57.8 %while.119 = (s32[]{:T(128)}, f32[1024,4,72]{0,2,1:T(8,128)S(1)}, f32[1024,4,72]{0,2,1:T(8,128)}, bf16[2,512,4,72]{1,0,3,2:T(2,128)(2,1)}, bf16[2,512,4,72]{1,3,...) while((s32[]{:T(128)}, f32[1024,4,72]{0,2,1:T(8,128)S(1)}, ...), condition=%wide.region_46.47_spmd.clone, body=%wide.region_44.46_spmd.clone.sunk | while | flops 1543175168 | bytes 160788816 | solution.py:442
  1100.2 11.7 dynamic_update_slice.173
  1128.5 11.7 dynamic_update_slice.173
  1166.2 58.0 %while.118 = (s32[]{:T(128)}, f32[1024,4,72]{0,2,1:T(8,128)S(1)}, f32[1024,4,72]{0,2,1:T(8,128)}, bf16[2,512,4,72]{1,0,3,2:T(2,128)(2,1)}, bf16[2,512,4,72]{1,3,...) while((s32[]{:T(128)}, f32[1024,4,72]{0,2,1:T(8,128)S(1)}, ...), condition=%wide.region_43.44_spmd.clone, body=%wide.region_41.43_spmd.clone.sunk | while | flops 1543175168 | bytes 160788816 | solution.py:442
  1175.3 11.8 dynamic_update_slice.172
  1203.6 11.8 dynamic_update_slice.172
  1250.3 6.0 collective-permute-start.110
  1263.7 14.2 collective-permute-done.110
  1284.3 14.8 collective-permute-done.115
  1300.3 19.8 %collective-permute-done.106 = bf16[432,1152]{1,0:T(8,128)(2,1)S(1)} collective-permute-done((bf16[432,1152]{1,0:T(8,128)(2,1)S(1)}, bf16[432,1152]{1,0:T(8,128)(2,1)S(1)}, u32[]{:S(2)}, u32[]{:S(2)}) %collective-permute-start.106) | collective-permute-done | bytes 995360 | tf_op jit(solution)/shard_map/ppermute | solution.py:269
  1323.7 5.8 broadcast_select_fusion.18
  1355.8 87.2 %collective-permute-done.69 = f32[2,16128]{1,0:T(2,128)S(1)} collective-permute-done((f32[2,16128]{1,0:T(2,128)S(1)}, f32[2,16128]{1,0:T(2,128)S(1)}, u32[]{:S(2)}, u32[]{:S(2)}) %collective-permute-start.69) | collective-permute-done | bytes 129056 | tf_op jit(solution)/shard_map/ppermute | solution.py:104
  1454.9 6.6 collective-permute-done.64
  1474.9 10.7 collective-permute-done.66
  1490.6 9.9 collective-permute-done.71
  1545.1 16.7 collective-permute-start.76
  1607.1 19.7 %collective-permute-done.88 = bf16[432,1152]{1,0:T(8,128)(2,1)} collective-permute-done((bf16[432,1152]{1,0:T(8,128)(2,1)}, bf16[432,1152]{1,0:T(8,128)(2,1)}, u32[]{:S(2)}, u32[]{:S(2)}) %collective-permute-start.88) | collective-permute-done | bytes 995360 | tf_op jit(solution)/shard_map/ppermute | solution.py:250
  1641.7 8.3 dynamic_update_slice.121
  1651.3 7.5 dynamic_update_slice.123
  1658.9 8.2 dynamic_update_slice.124
  1668.7 7.5 dynamic_update_slice.126
  1677.8 8.1 dynamic_update_slice.128
  1699.4 13.7 collective-permute-done.98
  1722.2 58.6 %collective-permute-done.91 = bf16[432,1152]{1,0:T(8,128)(2,1)S(1)} collective-permute-done((bf16[432,1152]{1,0:T(8,128)(2,1)S(1)}, bf16[432,1152]{1,0:T(8,128)(2,1)S(1)}, u32[]{:S(2)}, u32[]{:S(2)}) %collective-permute-start.91) | collective-permute-done | bytes 995360 | tf_op jit(solution)/shard_map/ppermute | solution.py:269
  1789.4 6.3 copy.223
  1822.9 15.8 fusion.183
  1838.7 14.7 fusion.184
  1853.5 11.6 fusion.178
  1865.1 14.5 fusion.182
  1884.9 7.6 multiply_subtract_fusion
  (1735 shorter events, 1007.7 us)
Async XLA Ops:
  19.4 216.8 %collective-permute-start.25 = (bf16[432,1152]{1,0:T(8,128)(2,1)}, bf16[432,1152]{1,0:T(8,128)(2,1)}, u32[]{:S(2)}, u32[]{:S(2)}) collective-permute-start(bf16[432,1152]{1,0:T(8,128)(2,1)} %get-tuple-element.1294), channel_id=1, source_target_pairs={{0,8},{8,16},{16,24},{1,9},{9,17},{17,25},{2,10},{10,18},{18,26},{... | collective-permute-start | bytes 2985992 | tf_op jit(solution)/shard_map/ppermute | solution.py:185
  25.2 211.6 %collective-permute-start.36 = (bf16[432,1152]{1,0:T(8,128)(2,1)}, bf16[432,1152]{1,0:T(8,128)(2,1)}, u32[]{:S(2)}, u32[]{:S(2)}) collective-permute-start(bf16[432,1152]{1,0:T(8,128)(2,1)} %get-tuple-element.1294), channel_id=1, source_target_pairs={{8,0},{16,8},{24,16},{9,1},{17,9},{25,17},{10,2},{18,10},{26,18},{... | collective-permute-start | bytes 2985992 | tf_op jit(solution)/shard_map/ppermute | solution.py:186
  26.5 215.4 %collective-permute-start.28 = (bf16[432,1152]{1,0:T(8,128)(2,1)}, bf16[432,1152]{1,0:T(8,128)(2,1)}, u32[]{:S(2)}, u32[]{:S(2)}) collective-permute-start(bf16[432,1152]{1,0:T(8,128)(2,1)} %get-tuple-element.1295), channel_id=1, source_target_pairs={{0,8},{8,16},{16,24},{1,9},{9,17},{17,25},{2,10},{10,18},{18,26},{... | collective-permute-start | bytes 2985992 | tf_op jit(solution)/shard_map/ppermute | solution.py:185
  32.8 58.7 %collective-permute-start.2 = (s32[1,4,2]{0,2,1:T(2,128)S(1)}, s32[1,4,2]{0,2,1:T(2,128)S(1)}, u32[]{:S(2)}, u32[]{:S(2)}) collective-permute-start(s32[1,4,2]{0,2,1:T(2,128)S(1)} %reshape.1039), channel_id=1, source_target_pairs={{0,4},{4,0},{1,5},{5,1},{2,6},{6,2},{3,7},{7,3},{8,12},{12,8},{9,1... | collective-permute-start | bytes 104 | tf_op jit(solution)/shard_map/ppermute | solution.py:104
  61.9 38.8 %collective-permute-start.5 = (bf16[603,128]{1,0:T(8,128)(2,1)S(1)}, bf16[603,128]{1,0:T(8,128)(2,1)}, u32[]{:S(2)}, u32[]{:S(2)}) collective-permute-start(bf16[603,128]{1,0:T(8,128)(2,1)S(1)} %concatenate.216), channel_id=1, source_target_pairs={{0,1},{1,0},{2,3},{3,2},{4,5},{5,4},{6,7},{7,6},{8,9},{9,8},{10,11... | collective-permute-start | bytes 463112 | tf_op jit(solution)/shard_map/ppermute | solution.py:104
  127.8 33.8 %collective-permute-start = (bf16[16,256]{1,0:T(8,128)(2,1)}, bf16[16,256]{1,0:T(8,128)(2,1)}, u32[]{:S(2)}, u32[]{:S(2)}) collective-permute-start(bf16[16,256]{1,0:T(8,128)(2,1)} %get-tuple-element.1340), channel_id=1, source_target_pairs={{0,2},{2,0},{1,3},{3,1},{4,6},{6,4},{5,7},{7,5},{8,10},{10,8},{9,1... | collective-permute-start | bytes 24584 | tf_op jit(solution)/shard_map/ppermute | solution.py:140
  169.8 73.8 %collective-permute-start.37 = (bf16[432,1152]{1,0:T(8,128)(2,1)}, bf16[432,1152]{1,0:T(8,128)(2,1)}, u32[]{:S(2)}, u32[]{:S(2)}) collective-permute-start(bf16[432,1152]{1,0:T(8,128)(2,1)} %get-tuple-element.1295), channel_id=1, source_target_pairs={{8,0},{16,8},{24,16},{9,1},{17,9},{25,17},{10,2},{18,10},{26,18},{... | collective-permute-start | bytes 2985992 | tf_op jit(solution)/shard_map/ppermute | solution.py:186
  171.2 24.9 %collective-permute-start.18 = (f32[16,1152]{1,0:T(8,128)S(1)}, f32[16,1152]{1,0:T(8,128)}, u32[]{:S(2)}, u32[]{:S(2)}) collective-permute-start(f32[16,1152]{1,0:T(8,128)S(1)} %add.1241), channel_id=1, source_target_pairs={{0,8},{8,0},{16,24},{24,16},{1,9},{9,1},{17,25},{25,17},{2,10},{10... | collective-permute-start | bytes 221192 | tf_op jit(solution)/shard_map/ppermute | solution.py:104
  236.9 27.2 %collective-permute-start.43 = (bf16[432,1152]{1,0:T(8,128)(2,1)}, bf16[432,1152]{1,0:T(8,128)(2,1)}, u32[]{:S(2)}, u32[]{:S(2)}) collective-permute-start(bf16[432,1152]{1,0:T(8,128)(2,1)} %collective-permute-done.36), channel_id=1, source_target_pairs={{8,0},{16,8},{9,1},{17,9},{10,2},{18,10},{11,3},{19,11},{12,4},{20... | collective-permute-start | bytes 2985992 | tf_op jit(solution)/shard_map/ppermute | solution.py:186
  240.3 25.0 %collective-permute-start.23 = (f32[1,16128]{1,0:T(1,128)S(1)}, f32[1,16128]{1,0:T(1,128)S(1)}, u32[]{:S(2)}, u32[]{:S(2)}) collective-permute-start(f32[1,16128]{1,0:T(1,128)S(1)} %constant_dynamic-slice_fusion.11), channel_id=1, source_target_pairs={{0,2},{2,0},{1,3},{3,1},{4,6},{6,4},{5,7},{7,5},{8,10},{10,8},{9,1... | collective-permute-start | bytes 193544 | tf_op jit(solution)/shard_map/ppermute | solution.py:104
  242.0 29.2 %collective-permute-start.29 = (bf16[432,1152]{1,0:T(8,128)(2,1)}, bf16[432,1152]{1,0:T(8,128)(2,1)}, u32[]{:S(2)}, u32[]{:S(2)}) collective-permute-start(bf16[432,1152]{1,0:T(8,128)(2,1)} %collective-permute-done.28), channel_id=1, source_target_pairs={{8,16},{16,24},{9,17},{17,25},{10,18},{18,26},{11,19},{19,27},{12,... | collective-permute-start | bytes 2985992 | tf_op jit(solution)/shard_map/ppermute | solution.py:185
  243.6 41.8 %collective-permute-start.44 = (bf16[432,1152]{1,0:T(8,128)(2,1)}, bf16[432,1152]{1,0:T(8,128)(2,1)}, u32[]{:S(2)}, u32[]{:S(2)}) collective-permute-start(bf16[432,1152]{1,0:T(8,128)(2,1)} %collective-permute-done.37), channel_id=1, source_target_pairs={{8,0},{16,8},{9,1},{17,9},{10,2},{18,10},{11,3},{19,11},{12,4},{20... | collective-permute-start | bytes 2985992 | tf_op jit(solution)/shard_map/ppermute | solution.py:186
  244.9 42.9 %collective-permute-start.27 = (bf16[432,1152]{1,0:T(8,128)(2,1)S(1)}, bf16[432,1152]{1,0:T(8,128)(2,1)}, u32[]{:S(2)}, u32[]{:S(2)}) collective-permute-start(bf16[432,1152]{1,0:T(8,128)(2,1)S(1)} %collective-permute-done.26), channel_id=1, source_target_pairs={{16,24},{17,25},{18,26},{19,27},{20,28},{21,29},{22,30},{23,31}} | collective-permute-start | bytes 2985992 | tf_op jit(solution)/shard_map/ppermute | solution.py:185
  264.1 42.7 %collective-permute-start.50 = (bf16[432,1152]{1,0:T(8,128)(2,1)}, bf16[432,1152]{1,0:T(8,128)(2,1)}, u32[]{:S(2)}, u32[]{:S(2)}) collective-permute-start(bf16[432,1152]{1,0:T(8,128)(2,1)} %collective-permute-done.43), channel_id=1, source_target_pairs={{8,0},{9,1},{10,2},{11,3},{12,4},{13,5},{14,6},{15,7}} | collective-permute-start | bytes 2985992 | tf_op jit(solution)/shard_map/ppermute | solution.py:186
  271.1 41.5 %collective-permute-start.30 = (bf16[432,1152]{1,0:T(8,128)(2,1)}, bf16[432,1152]{1,0:T(8,128)(2,1)S(1)}, u32[]{:S(2)}, u32[]{:S(2)}) collective-permute-start(bf16[432,1152]{1,0:T(8,128)(2,1)} %collective-permute-done.29), channel_id=1, source_target_pairs={{16,24},{17,25},{18,26},{19,27},{20,28},{21,29},{22,30},{23,31}} | collective-permute-start | bytes 2985992 | tf_op jit(solution)/shard_map/ppermute | solution.py:185
  285.4 40.4 %collective-permute-start.51 = (bf16[432,1152]{1,0:T(8,128)(2,1)}, bf16[432,1152]{1,0:T(8,128)(2,1)S(1)}, u32[]{:S(2)}, u32[]{:S(2)}) collective-permute-start(bf16[432,1152]{1,0:T(8,128)(2,1)} %collective-permute-done.44), channel_id=1, source_target_pairs={{8,0},{9,1},{10,2},{11,3},{12,4},{13,5},{14,6},{15,7}} | collective-permute-start | bytes 2985992 | tf_op jit(solution)/shard_map/ppermute | solution.py:186
  310.5 50.6 %collective-permute-start.45 = (bf16[432,1152]{1,0:T(8,128)(2,1)S(1)}, bf16[432,1152]{1,0:T(8,128)(2,1)S(1)}, u32[]{:S(2)}, u32[]{:S(2)}) collective-permute-start(bf16[432,1152]{1,0:T(8,128)(2,1)S(1)} %get-tuple-element.1227), channel_id=1, source_target_pairs={{0,2},{2,0},{1,3},{3,1},{4,6},{6,4},{5,7},{7,5},{8,10},{10,8},{9,1... | collective-permute-start | bytes 2985992 | tf_op jit(solution)/shard_map/ppermute | solution.py:200
  311.4 45.4 %collective-permute-start.31 = (bf16[432,1152]{1,0:T(8,128)(2,1)S(1)}, bf16[432,1152]{1,0:T(8,128)(2,1)S(1)}, u32[]{:S(2)}, u32[]{:S(2)}) collective-permute-start(bf16[432,1152]{1,0:T(8,128)(2,1)S(1)} %get-tuple-element.1229), channel_id=1, source_target_pairs={{0,2},{2,0},{1,3},{3,1},{4,6},{6,4},{5,7},{7,5},{8,10},{10,8},{9,1... | collective-permute-start | bytes 2985992 | tf_op jit(solution)/shard_map/ppermute | solution.py:200
  329.9 33.5 %collective-permute-start.33 = (bf16[432,1152]{1,0:T(8,128)(2,1)S(1)}, bf16[432,1152]{1,0:T(8,128)(2,1)S(1)}, u32[]{:S(2)}, u32[]{:S(2)}) collective-permute-start(bf16[432,1152]{1,0:T(8,128)(2,1)S(1)} %get-tuple-element.1233), channel_id=1, source_target_pairs={{0,4},{4,0},{1,5},{5,1},{2,6},{6,2},{3,7},{7,3},{8,12},{12,8},{9,1... | collective-permute-start | bytes 2985992 | tf_op jit(solution)/shard_map/ppermute | solution.py:202
  331.7 46.4 %collective-permute-start.38 = (bf16[432,1152]{1,0:T(8,128)(2,1)S(1)}, bf16[432,1152]{1,0:T(8,128)(2,1)S(1)}, u32[]{:S(2)}, u32[]{:S(2)}) collective-permute-start(bf16[432,1152]{1,0:T(8,128)(2,1)S(1)} %get-tuple-element.1228), channel_id=1, source_target_pairs={{0,2},{2,0},{1,3},{3,1},{4,6},{6,4},{5,7},{7,5},{8,10},{10,8},{9,1... | collective-permute-start | bytes 2985992 | tf_op jit(solution)/shard_map/ppermute | solution.py:200
  357.0 70.0 %collective-permute-start.32 = (bf16[2,432,1152]{2,1,0:T(8,128)(2,1)S(1)}, bf16[2,432,1152]{2,1,0:T(8,128)(2,1)S(1)}, u32[]{:S(2)}, u32[]{:S(2)}) collective-permute-start(bf16[2,432,1152]{2,1,0:T(8,128)(2,1)S(1)} %pad_maximum_fusion.9), channel_id=1, source_target_pairs={{0,4},{4,0},{1,5},{5,1},{2,6},{6,2},{3,7},{7,3},{8,12},{12,8},{9,1... | collective-permute-start | bytes 5971976 | tf_op jit(solution)/shard_map/ppermute | solution.py:201
  359.7 65.0 %collective-permute-start.40 = (bf16[432,1152]{1,0:T(8,128)(2,1)S(1)}, bf16[432,1152]{1,0:T(8,128)(2,1)S(1)}, u32[]{:S(2)}, u32[]{:S(2)}) collective-permute-start(bf16[432,1152]{1,0:T(8,128)(2,1)S(1)} %get-tuple-element.1232), channel_id=1, source_target_pairs={{0,4},{4,0},{1,5},{5,1},{2,6},{6,2},{3,7},{7,3},{8,12},{12,8},{9,1... | collective-permute-start | bytes 2985992 | tf_op jit(solution)/shard_map/ppermute | solution.py:202
  361.1 174.5 %collective-permute-start.52 = (bf16[432,1152]{1,0:T(8,128)(2,1)}, bf16[432,1152]{1,0:T(8,128)(2,1)}, u32[]{:S(2)}, u32[]{:S(2)}) collective-permute-start(bf16[432,1152]{1,0:T(8,128)(2,1)} %get-tuple-element.1226), channel_id=1, source_target_pairs={{0,2},{2,0},{1,3},{3,1},{4,6},{6,4},{5,7},{7,5},{8,10},{10,8},{9,1... | collective-permute-start | bytes 2985992 | tf_op jit(solution)/shard_map/ppermute | solution.py:200
  363.5 176.2 %collective-permute-start.54 = (bf16[432,1152]{1,0:T(8,128)(2,1)}, bf16[432,1152]{1,0:T(8,128)(2,1)}, u32[]{:S(2)}, u32[]{:S(2)}) collective-permute-start(bf16[432,1152]{1,0:T(8,128)(2,1)} %get-tuple-element.1230), channel_id=1, source_target_pairs={{0,4},{4,0},{1,5},{5,1},{2,6},{6,2},{3,7},{7,3},{8,12},{12,8},{9,1... | collective-permute-start | bytes 2985992 | tf_op jit(solution)/shard_map/ppermute | solution.py:202
  378.2 119.4 %collective-permute-start.47 = (bf16[432,1152]{1,0:T(8,128)(2,1)}, bf16[432,1152]{1,0:T(8,128)(2,1)}, u32[]{:S(2)}, u32[]{:S(2)}) collective-permute-start(bf16[432,1152]{1,0:T(8,128)(2,1)} %get-tuple-element.1231), channel_id=1, source_target_pairs={{0,4},{4,0},{1,5},{5,1},{2,6},{6,2},{3,7},{7,3},{8,12},{12,8},{9,1... | collective-permute-start | bytes 2985992 | tf_op jit(solution)/shard_map/ppermute | solution.py:202
  424.7 43.5 %collective-permute-start.34 = (bf16[2,432,1152]{2,1,0:T(8,128)(2,1)}, bf16[2,432,1152]{2,1,0:T(8,128)(2,1)}, u32[]{:S(2)}, u32[]{:S(2)}) collective-permute-start(bf16[2,432,1152]{2,1,0:T(8,128)(2,1)} %pad_maximum_fusion.11), channel_id=1, source_target_pairs={{0,2},{2,0},{1,3},{3,1},{4,6},{6,4},{5,7},{7,5},{8,10},{10,8},{9,1... | collective-permute-start | bytes 5971976 | tf_op jit(solution)/shard_map/ppermute | solution.py:203
  427.1 74.3 %collective-permute-start.39 = (bf16[2,432,1152]{2,1,0:T(8,128)(2,1)}, bf16[2,432,1152]{2,1,0:T(8,128)(2,1)}, u32[]{:S(2)}, u32[]{:S(2)}) collective-permute-start(bf16[2,432,1152]{2,1,0:T(8,128)(2,1)} %pad_maximum_fusion.15), channel_id=1, source_target_pairs={{0,4},{4,0},{1,5},{5,1},{2,6},{6,2},{3,7},{7,3},{8,12},{12,8},{9,1... | collective-permute-start | bytes 5971976 | tf_op jit(solution)/shard_map/ppermute | solution.py:201
  468.2 37.8 %collective-permute-start.41 = (bf16[2,432,1152]{2,1,0:T(8,128)(2,1)}, bf16[2,432,1152]{2,1,0:T(8,128)(2,1)}, u32[]{:S(2)}, u32[]{:S(2)}) collective-permute-start(bf16[2,432,1152]{2,1,0:T(8,128)(2,1)} %pad_maximum_fusion.17), channel_id=1, source_target_pairs={{0,2},{2,0},{1,3},{3,1},{4,6},{6,4},{5,7},{7,5},{8,10},{10,8},{9,1... | collective-permute-start | bytes 5971976 | tf_op jit(solution)/shard_map/ppermute | solution.py:203
  502.6 46.3 %collective-permute-start.46 = (bf16[2,432,1152]{2,1,0:T(8,128)(2,1)S(1)}, bf16[2,432,1152]{2,1,0:T(8,128)(2,1)S(1)}, u32[]{:S(2)}, u32[]{:S(2)}) collective-permute-start(bf16[2,432,1152]{2,1,0:T(8,128)(2,1)S(1)} %copy-done.217), channel_id=1, source_target_pairs={{0,4},{4,0},{1,5},{5,1},{2,6},{6,2},{3,7},{7,3},{8,12},{12,8},{9,1... | collective-permute-start | bytes 5971976 | tf_op jit(solution)/shard_map/ppermute | solution.py:201
  506.1 47.0 %collective-permute-start.48 = (bf16[2,432,1152]{2,1,0:T(8,128)(2,1)S(1)}, bf16[2,432,1152]{2,1,0:T(8,128)(2,1)}, u32[]{:S(2)}, u32[]{:S(2)}) collective-permute-start(bf16[2,432,1152]{2,1,0:T(8,128)(2,1)S(1)} %pad_maximum_fusion.23), channel_id=1, source_target_pairs={{0,2},{2,0},{1,3},{3,1},{4,6},{6,4},{5,7},{7,5},{8,10},{10,8},{9,1... | collective-permute-start | bytes 5971976 | tf_op jit(solution)/shard_map/ppermute | solution.py:203
  539.3 68.0 %collective-permute-start.53 = (bf16[2,432,1152]{2,1,0:T(8,128)(2,1)}, bf16[2,432,1152]{2,1,0:T(8,128)(2,1)}, u32[]{:S(2)}, u32[]{:S(2)}) collective-permute-start(bf16[2,432,1152]{2,1,0:T(8,128)(2,1)} %pad_maximum_fusion.27), channel_id=1, source_target_pairs={{0,4},{4,0},{1,5},{5,1},{2,6},{6,2},{3,7},{7,3},{8,12},{12,8},{9,1... | collective-permute-start | bytes 5971976 | tf_op jit(solution)/shard_map/ppermute | solution.py:201
  542.6 67.2 %collective-permute-start.55 = (bf16[2,432,1152]{2,1,0:T(8,128)(2,1)}, bf16[2,432,1152]{2,1,0:T(8,128)(2,1)}, u32[]{:S(2)}, u32[]{:S(2)}) collective-permute-start(bf16[2,432,1152]{2,1,0:T(8,128)(2,1)} %pad_maximum_fusion.29), channel_id=1, source_target_pairs={{0,2},{2,0},{1,3},{3,1},{4,6},{6,4},{5,7},{7,5},{8,10},{10,8},{9,1... | collective-permute-start | bytes 5971976 | tf_op jit(solution)/shard_map/ppermute | solution.py:203
  815.2 86.2 %collective-permute-start.100 = (bf16[2,432,1152]{2,1,0:T(8,128)(2,1)}, bf16[2,432,1152]{2,1,0:T(8,128)(2,1)}, u32[]{:S(2)}, u32[]{:S(2)}) collective-permute-start(bf16[2,432,1152]{2,1,0:T(8,128)(2,1)} %pad_maximum_fusion.36), channel_id=1, source_target_pairs={{0,2},{2,0},{1,3},{3,1},{4,6},{6,4},{5,7},{7,5},{8,10},{10,8},{9,1... | collective-permute-start | bytes 5971976 | tf_op jit(solution)/shard_map/ppermute | solution.py:243
  817.6 86.2 %collective-permute-start.108 = (bf16[2,432,1152]{2,1,0:T(8,128)(2,1)}, bf16[2,432,1152]{2,1,0:T(8,128)(2,1)}, u32[]{:S(2)}, u32[]{:S(2)}) collective-permute-start(bf16[2,432,1152]{2,1,0:T(8,128)(2,1)} %pad_maximum_fusion.38), channel_id=1, source_target_pairs={{0,2},{2,0},{1,3},{3,1},{4,6},{6,4},{5,7},{7,5},{8,10},{10,8},{9,1... | collective-permute-start | bytes 5971976 | tf_op jit(solution)/shard_map/ppermute | solution.py:243
  911.3 134.6 %collective-permute-start.113 = (bf16[2,432,1152]{2,1,0:T(8,128)(2,1)}, bf16[2,432,1152]{2,1,0:T(8,128)(2,1)}, u32[]{:S(2)}, u32[]{:S(2)}) collective-permute-start(bf16[2,432,1152]{2,1,0:T(8,128)(2,1)} %pad_maximum_fusion.39), channel_id=1, source_target_pairs={{0,4},{4,0},{1,5},{5,1},{2,6},{6,2},{3,7},{7,3},{8,12},{12,8},{9,1... | collective-permute-start | bytes 5971976 | tf_op jit(solution)/shard_map/ppermute | solution.py:248
  914.6 135.1 %collective-permute-start.104 = (bf16[2,432,1152]{2,1,0:T(8,128)(2,1)}, bf16[2,432,1152]{2,1,0:T(8,128)(2,1)}, u32[]{:S(2)}, u32[]{:S(2)}) collective-permute-start(bf16[2,432,1152]{2,1,0:T(8,128)(2,1)} %pad_maximum_fusion.37), channel_id=1, source_target_pairs={{0,4},{4,0},{1,5},{5,1},{2,6},{6,2},{3,7},{7,3},{8,12},{12,8},{9,1... | collective-permute-start | bytes 5971976 | tf_op jit(solution)/shard_map/ppermute | solution.py:248
  914.8 329.0 %collective-permute-start.109 = (bf16[432,1152]{1,0:T(8,128)(2,1)}, bf16[432,1152]{1,0:T(8,128)(2,1)}, u32[]{:S(2)}, u32[]{:S(2)}) collective-permute-start(bf16[432,1152]{1,0:T(8,128)(2,1)} %get-tuple-element.1249), channel_id=1, source_target_pairs={{0,4},{4,0},{1,5},{5,1},{2,6},{6,2},{3,7},{7,3},{8,12},{12,8},{9,1... | collective-permute-start | bytes 2985992 | tf_op jit(solution)/shard_map/ppermute | solution.py:245
  916.6 125.2 %collective-permute-start.101 = (bf16[432,1152]{1,0:T(8,128)(2,1)}, bf16[432,1152]{1,0:T(8,128)(2,1)}, u32[]{:S(2)}, u32[]{:S(2)}) collective-permute-start(bf16[432,1152]{1,0:T(8,128)(2,1)} %get-tuple-element.1277), channel_id=1, source_target_pairs={{0,4},{4,0},{1,5},{5,1},{2,6},{6,2},{3,7},{7,3},{8,12},{12,8},{9,1... | collective-permute-start | bytes 2985992 | tf_op jit(solution)/shard_map/ppermute | solution.py:245
  972.2 97.0 %collective-permute-start.61 = (bf16[1024,1152]{1,0:T(8,128)(2,1)}, bf16[1024,1152]{1,0:T(8,128)(2,1)}, u32[]{:S(2)}, u32[]{:S(2)}) collective-permute-start(bf16[1024,1152]{1,0:T(8,128)(2,1)} %add_convert_fusion.1), channel_id=1, source_target_pairs={{0,1},{1,0},{2,3},{3,2},{4,5},{5,4},{6,7},{7,6},{8,9},{9,8},{10,11... | collective-permute-start | bytes 7077896 | tf_op jit(solution)/shard_map/ppermute | solution.py:452
  1048.8 196.3 %collective-permute-start.114 = (bf16[432,1152]{1,0:T(8,128)(2,1)}, bf16[432,1152]{1,0:T(8,128)(2,1)}, u32[]{:S(2)}, u32[]{:S(2)}) collective-permute-start(bf16[432,1152]{1,0:T(8,128)(2,1)} %fusion.232), channel_id=1, source_target_pairs={{0,2},{2,0},{1,3},{3,1},{4,6},{6,4},{5,7},{7,5},{8,10},{10,8},{9,1... | collective-permute-start | bytes 2985992 | tf_op jit(solution)/shard_map/ppermute | solution.py:250
  1052.5 192.6 %collective-permute-start.105 = (bf16[432,1152]{1,0:T(8,128)(2,1)}, bf16[432,1152]{1,0:T(8,128)(2,1)}, u32[]{:S(2)}, u32[]{:S(2)}) collective-permute-start(bf16[432,1152]{1,0:T(8,128)(2,1)} %fusion.236), channel_id=1, source_target_pairs={{0,2},{2,0},{1,3},{3,1},{4,6},{6,4},{5,7},{7,5},{8,10},{10,8},{9,1... | collective-permute-start | bytes 2985992 | tf_op jit(solution)/shard_map/ppermute | solution.py:250
  1067.4 192.0 %collective-permute-start.103 = (bf16[432,1152]{1,0:T(8,128)(2,1)}, bf16[432,1152]{1,0:T(8,128)(2,1)}, u32[]{:S(2)}, u32[]{:S(2)}) collective-permute-start(bf16[432,1152]{1,0:T(8,128)(2,1)} %add_convert_fusion.27), channel_id=1, source_target_pairs={{8,16},{9,17},{10,18},{11,19},{12,20},{13,21},{14,22},{15,23}} | collective-permute-start | bytes 2985992 | tf_op jit(solution)/shard_map/ppermute | solution.py:269
  1161.8 160.2 %collective-permute-start.82 = (bf16[2,432,1152]{2,1,0:T(8,128)(2,1)}, bf16[2,432,1152]{2,1,0:T(8,128)(2,1)}, u32[]{:S(2)}, u32[]{:S(2)}) collective-permute-start(bf16[2,432,1152]{2,1,0:T(8,128)(2,1)} %pad_maximum_fusion.32), channel_id=1, source_target_pairs={{0,2},{2,0},{1,3},{3,1},{4,6},{6,4},{5,7},{7,5},{8,10},{10,8},{9,1... | collective-permute-start | bytes 5971976 | tf_op jit(solution)/shard_map/ppermute | solution.py:243
  1243.8 79.8 %collective-permute-start.92 = (bf16[2,432,1152]{2,1,0:T(8,128)(2,1)}, bf16[2,432,1152]{2,1,0:T(8,128)(2,1)}, u32[]{:S(2)}, u32[]{:S(2)}) collective-permute-start(bf16[2,432,1152]{2,1,0:T(8,128)(2,1)} %pad_maximum_fusion.34), channel_id=1, source_target_pairs={{0,2},{2,0},{1,3},{3,1},{4,6},{6,4},{5,7},{7,5},{8,10},{10,8},{9,1... | collective-permute-start | bytes 5971976 | tf_op jit(solution)/shard_map/ppermute | solution.py:243
  1245.1 92.9 %collective-permute-start.62 = (bf16[1024,1152]{1,0:T(8,128)(2,1)S(1)}, bf16[1024,1152]{1,0:T(8,128)(2,1)}, u32[]{:S(2)}, u32[]{:S(2)}) collective-permute-start(bf16[1024,1152]{1,0:T(8,128)(2,1)S(1)} %add_convert_fusion), channel_id=1, source_target_pairs={{0,1},{1,0},{2,3},{3,2},{4,5},{5,4},{6,7},{7,6},{8,9},{9,8},{10,11... | collective-permute-start | bytes 7077896 | tf_op jit(solution)/shard_map/ppermute | solution.py:452
  1250.3 27.6 %collective-permute-start.110 = (bf16[432,1152]{1,0:T(8,128)(2,1)}, bf16[432,1152]{1,0:T(8,128)(2,1)}, u32[]{:S(2)}, u32[]{:S(2)}) collective-permute-start(bf16[432,1152]{1,0:T(8,128)(2,1)} %get-tuple-element.1246), channel_id=1, source_target_pairs={{0,8},{1,9},{2,10},{3,11},{4,12},{5,13},{6,14},{7,15}} | collective-permute-start | bytes 2985992 | tf_op jit(solution)/shard_map/ppermute | solution.py:269
  1259.4 39.7 %collective-permute-start.115 = (bf16[432,1152]{1,0:T(8,128)(2,1)S(1)}, bf16[432,1152]{1,0:T(8,128)(2,1)S(1)}, u32[]{:S(2)}, u32[]{:S(2)}) collective-permute-start(bf16[432,1152]{1,0:T(8,128)(2,1)S(1)} %copy-done.165), channel_id=1, source_target_pairs={{0,8},{1,9},{2,10},{3,11},{4,12},{5,13},{6,14},{7,15}} | collective-permute-start | bytes 2985992 | tf_op jit(solution)/shard_map/ppermute | solution.py:269
  1277.9 42.2 %collective-permute-start.106 = (bf16[432,1152]{1,0:T(8,128)(2,1)S(1)}, bf16[432,1152]{1,0:T(8,128)(2,1)S(1)}, u32[]{:S(2)}, u32[]{:S(2)}) collective-permute-start(bf16[432,1152]{1,0:T(8,128)(2,1)S(1)} %get-tuple-element.1247), channel_id=1, source_target_pairs={{0,8},{24,16},{1,9},{25,17},{2,10},{26,18},{3,11},{27,19},{4,12},{... | collective-permute-start | bytes 2985992 | tf_op jit(solution)/shard_map/ppermute | solution.py:269
  1299.1 35.2 %collective-permute-start.111 = (bf16[432,1152]{1,0:T(8,128)(2,1)S(1)}, bf16[432,1152]{1,0:T(8,128)(2,1)S(1)}, u32[]{:S(2)}, u32[]{:S(2)}) collective-permute-start(bf16[432,1152]{1,0:T(8,128)(2,1)S(1)} %add_convert_fusion.21), channel_id=1, source_target_pairs={{8,16},{9,17},{10,18},{11,19},{12,20},{13,21},{14,22},{15,23}} | collective-permute-start | bytes 2985992 | tf_op jit(solution)/shard_map/ppermute | solution.py:269
  1322.0 121.2 %collective-permute-start.107 = (bf16[432,1152]{1,0:T(8,128)(2,1)}, bf16[432,1152]{1,0:T(8,128)(2,1)}, u32[]{:S(2)}, u32[]{:S(2)}) collective-permute-start(bf16[432,1152]{1,0:T(8,128)(2,1)} %add_convert_fusion.24), channel_id=1, source_target_pairs={{8,16},{9,17},{10,18},{11,19},{12,20},{13,21},{14,22},{15,23}} | collective-permute-start | bytes 2985992 | tf_op jit(solution)/shard_map/ppermute | solution.py:269
  1331.0 247.0 %collective-permute-start.96 = (bf16[2,432,1152]{2,1,0:T(8,128)(2,1)}, bf16[2,432,1152]{2,1,0:T(8,128)(2,1)}, u32[]{:S(2)}, u32[]{:S(2)}) collective-permute-start(bf16[2,432,1152]{2,1,0:T(8,128)(2,1)} %pad_maximum_fusion.35), channel_id=1, source_target_pairs={{0,4},{4,0},{1,5},{5,1},{2,6},{6,2},{3,7},{7,3},{8,12},{12,8},{9,1... | collective-permute-start | bytes 5971976 | tf_op jit(solution)/shard_map/ppermute | solution.py:248
  1334.3 247.9 %collective-permute-start.87 = (bf16[2,432,1152]{2,1,0:T(8,128)(2,1)}, bf16[2,432,1152]{2,1,0:T(8,128)(2,1)}, u32[]{:S(2)}, u32[]{:S(2)}) collective-permute-start(bf16[2,432,1152]{2,1,0:T(8,128)(2,1)} %pad_maximum_fusion.33), channel_id=1, source_target_pairs={{0,4},{4,0},{1,5},{5,1},{2,6},{6,2},{3,7},{7,3},{8,12},{12,8},{9,1... | collective-permute-start | bytes 5971976 | tf_op jit(solution)/shard_map/ppermute | solution.py:248
  1335.0 127.6 %collective-permute-start.83 = (bf16[432,1152]{1,0:T(8,128)(2,1)}, bf16[432,1152]{1,0:T(8,128)(2,1)}, u32[]{:S(2)}, u32[]{:S(2)}) collective-permute-start(bf16[432,1152]{1,0:T(8,128)(2,1)} %get-tuple-element.1275), channel_id=1, source_target_pairs={{0,4},{4,0},{1,5},{5,1},{2,6},{6,2},{3,7},{7,3},{8,12},{12,8},{9,1... | collective-permute-start | bytes 2985992 | tf_op jit(solution)/shard_map/ppermute | solution.py:245
  1355.4 87.6 %collective-permute-start.69 = (f32[2,16128]{1,0:T(2,128)S(1)}, f32[2,16128]{1,0:T(2,128)S(1)}, u32[]{:S(2)}, u32[]{:S(2)}) collective-permute-start(f32[2,16128]{1,0:T(2,128)S(1)} %maximum_select_fusion.6), channel_id=1, source_target_pairs={{0,4},{4,0},{1,5},{5,1},{2,6},{6,2},{3,7},{7,3},{8,12},{12,8},{9,1... | collective-permute-start | bytes 387080 | tf_op jit(solution)/shard_map/ppermute | solution.py:104
  1469.3 137.7 %collective-permute-start.93 = (bf16[432,1152]{1,0:T(8,128)(2,1)}, bf16[432,1152]{1,0:T(8,128)(2,1)}, u32[]{:S(2)}, u32[]{:S(2)}) collective-permute-start(bf16[432,1152]{1,0:T(8,128)(2,1)} %get-tuple-element.1263), channel_id=1, source_target_pairs={{0,4},{4,0},{1,5},{5,1},{2,6},{6,2},{3,7},{7,3},{8,12},{12,8},{9,1... | collective-permute-start | bytes 2985992 | tf_op jit(solution)/shard_map/ppermute | solution.py:245
  1471.1 29.3 %collective-permute-start.71 = (f32[8,16128]{1,0:T(8,128)S(1)}, f32[8,16128]{1,0:T(8,128)S(1)}, u32[]{:S(2)}, u32[]{:S(2)}) collective-permute-start(f32[8,16128]{1,0:T(8,128)S(1)} %maximum_select_fusion.4), channel_id=1, source_target_pairs={{0,16},{8,24},{16,0},{24,8},{1,17},{9,25},{17,1},{25,9},{2,18},{10... | collective-permute-start | bytes 1548296 | tf_op jit(solution)/shard_map/ppermute | solution.py:104
  1485.7 50.6 %collective-permute-start.67 = (f32[460,128]{1,0:T(8,128)S(1)}, f32[460,128]{1,0:T(8,128)S(1)}, u32[]{:S(2)}, u32[]{:S(2)}) collective-permute-start(f32[460,128]{1,0:T(8,128)S(1)} %add.1371), channel_id=1, source_target_pairs={{0,16},{8,24},{16,0},{24,8},{1,17},{9,25},{17,1},{25,9},{2,18},{10... | collective-permute-start | bytes 706568 | tf_op jit(solution)/shard_map/ppermute | solution.py:104
  1534.3 66.8 %collective-permute-start.84 = (bf16[432,1152]{1,0:T(8,128)(2,1)}, bf16[432,1152]{1,0:T(8,128)(2,1)}, u32[]{:S(2)}, u32[]{:S(2)}) collective-permute-start(bf16[432,1152]{1,0:T(8,128)(2,1)} %add_convert_fusion.42), channel_id=1, source_target_pairs={{24,16},{25,17},{26,18},{27,19},{28,20},{29,21},{30,22},{31,23}} | collective-permute-start | bytes 2985992 | tf_op jit(solution)/shard_map/ppermute | solution.py:269
  1581.0 26.0 %collective-permute-start.97 = (bf16[432,1152]{1,0:T(8,128)(2,1)}, bf16[432,1152]{1,0:T(8,128)(2,1)}, u32[]{:S(2)}, u32[]{:S(2)}) collective-permute-start(bf16[432,1152]{1,0:T(8,128)(2,1)} %fusion.240), channel_id=1, source_target_pairs={{0,2},{2,0},{1,3},{3,1},{4,6},{6,4},{5,7},{7,5},{8,10},{10,8},{9,1... | collective-permute-start | bytes 2985992 | tf_op jit(solution)/shard_map/ppermute | solution.py:250
  1585.1 41.6 %collective-permute-start.88 = (bf16[432,1152]{1,0:T(8,128)(2,1)}, bf16[432,1152]{1,0:T(8,128)(2,1)}, u32[]{:S(2)}, u32[]{:S(2)}) collective-permute-start(bf16[432,1152]{1,0:T(8,128)(2,1)} %fusion.244), channel_id=1, source_target_pairs={{0,2},{2,0},{1,3},{3,1},{4,6},{6,4},{5,7},{7,5},{8,10},{10,8},{9,1... | collective-permute-start | bytes 2985992 | tf_op jit(solution)/shard_map/ppermute | solution.py:250
  1603.7 89.2 %collective-permute-start.85 = (bf16[432,1152]{1,0:T(8,128)(2,1)}, bf16[432,1152]{1,0:T(8,128)(2,1)}, u32[]{:S(2)}, u32[]{:S(2)}) collective-permute-start(bf16[432,1152]{1,0:T(8,128)(2,1)} %add_convert_fusion.41), channel_id=1, source_target_pairs={{16,8},{17,9},{18,10},{19,11},{20,12},{21,13},{22,14},{23,15}} | collective-permute-start | bytes 2985992 | tf_op jit(solution)/shard_map/ppermute | solution.py:269
  1632.5 63.4 %collective-permute-start.94 = (bf16[432,1152]{1,0:T(8,128)(2,1)}, bf16[432,1152]{1,0:T(8,128)(2,1)}, u32[]{:S(2)}, u32[]{:S(2)}) collective-permute-start(bf16[432,1152]{1,0:T(8,128)(2,1)} %get-tuple-element.1260), channel_id=1, source_target_pairs={{0,8},{24,16},{1,9},{25,17},{2,10},{26,18},{3,11},{27,19},{4,12},{... | collective-permute-start | bytes 2985992 | tf_op jit(solution)/shard_map/ppermute | solution.py:269
  1694.6 25.2 %collective-permute-start.86 = (bf16[432,1152]{1,0:T(8,128)(2,1)S(1)}, bf16[432,1152]{1,0:T(8,128)(2,1)S(1)}, u32[]{:S(2)}, u32[]{:S(2)}) collective-permute-start(bf16[432,1152]{1,0:T(8,128)(2,1)S(1)} %add_convert_fusion.40), channel_id=1, source_target_pairs={{8,0},{9,1},{10,2},{11,3},{12,4},{13,5},{14,6},{15,7}} | collective-permute-start | bytes 2985992 | tf_op jit(solution)/shard_map/ppermute | solution.py:269
  1720.3 60.5 %collective-permute-start.91 = (bf16[432,1152]{1,0:T(8,128)(2,1)S(1)}, bf16[432,1152]{1,0:T(8,128)(2,1)S(1)}, u32[]{:S(2)}, u32[]{:S(2)}) collective-permute-start(bf16[432,1152]{1,0:T(8,128)(2,1)S(1)} %add_convert_fusion.36), channel_id=1, source_target_pairs={{8,0},{9,1},{10,2},{11,3},{12,4},{13,5},{14,6},{15,7}} | collective-permute-start | bytes 2985992 | tf_op jit(solution)/shard_map/ppermute | solution.py:269
  (501 other events, 5805.0 us)
where the time goes:
time: 1910 us; the launch traced here: 1890 us
  waiting for transfers between devices  616 us (32%)
  matrix products  411 us (22%)
  local copies, waits for them, and re-layouts  378 us (20%)
  other arithmetic  313 us (16%)
  starting transfers between devices  156 us (8%)
    ppermute x47, waiting for transfers between devices, swap_by(): return lax.ppermute(value, axis, [(i, i ^ bit) for i in range(size)])  223 us
    ppermute x20, waiting for transfers between devices, reduce_line(): part = add_low(part, lax.ppermute(part, 'z', pairs))  139 us
    dynamic_update_slice x16, local copies, waits for them, and re-layouts, attend_forward(): lax.map(one_block, query.reshape(rows // block, block, heads, HD))  97.7 us
    dot_general x17, matrix products, contract_cols(): lax.dot_general(left, right, (((1,), (1,)), ((), ())), preferred_element_...  76.9 us
    ppermute x4, waiting for transfers between devices, reduce_plane(): got = lax.ppermute(pick(upper, False), 'y', SWAP)  63.8 us
    ppermute x6, waiting for transfers between devices, gather_strips(): lax.ppermute(left[-1], 'z', [(i + 1, i) for i in range(3 - hop)])  63.3 us
    ppermute x47, starting transfers between devices, swap_by(): return lax.ppermute(value, axis, [(i, i ^ bit) for i in range(size)])  59 us
    dot_general x18, matrix products, contract_rows(): lax.dot_general(left, right, (((0,), (0,)), ((), ())), preferred_element_...  53.8 us
  transfers between devices with their start and end apart: 123, of which 53 were waited for; matrix products, arithmetic and copies ran while one was open for 42% of the time, Pallas kernels for 0%

commit v1 on v0

v1 whole, which is shorter than its diff:
```python
import functools
import math

import jax
import jax.numpy as jnp
from jax import lax
from jax.experimental import pallas as pl
from jax.experimental.pallas import tpu as pltpu
from jax.sharding import Mesh
from jax.sharding import PartitionSpec as P

D = 1152
HD = 72
FF = 4608
PATCH = 16
FREQ = 256
CLASSES = 1000
BLK = 288
LAYERS = 2
STEP_COUNT = 10
MB = 2
SIDE = 32
LANE = 128
STRIP = 3 * BLK


HIGH = lax.Precision.HIGHEST
NORM_EPS = 1e-06
CLIP_AT = 0.005
ADAM_ONE = 0.9
ADAM_TWO = 0.999
ADAM_EPS = 1e-08
ADAM_RATE = 0.02
ADAM_DECAY = 0.01
SHAMPOO_ONE = 0.9
SHAMPOO_TWO = 0.99
SHAMPOO_RATE = 0.01
SHAMPOO_DECAY = 0.01

F32 = jnp.float32
BF16 = jnp.bfloat16
SWAP = [(0, 1), (1, 0)]
LOG2E = 1.4426950408889634
SCALE = HD ** (-0.5)
SC2 = SCALE * LOG2E
HEADS_HERE = 4
WIDE = HD * HEADS_HERE

ROW_D = D // LANE
ROW_STEM = (PATCH + 1) * ROW_D
BASE_W1 = ROW_STEM
BASE_B1 = BASE_W1 + FREQ * ROW_D
BASE_W2 = BASE_B1 + ROW_D
BASE_B2 = BASE_W2 + D * ROW_D
BASE_TABLE = BASE_B2 + ROW_D
BASE_LAYER = BASE_TABLE + CLASSES * ROW_D
ROW_ADA = 6 * ROW_D
ROW_BIAS = (6 + 3 + 1 + 4 + 1) * ROW_D
LAYER_ROWS = D * ROW_ADA + ROW_BIAS
BASE_FINAL = BASE_LAYER + LAYERS * LAYER_ROWS
ROW_FINAL = 2 * ROW_D
BASE_TAIL = BASE_FINAL + D * ROW_FINAL
ROW_TAIL = ROW_FINAL + PATCH * ROW_D
FRONT = 56


def time_freq(step):
    half = FREQ // 2
    freqs = jnp.exp(-math.log(10000.0) * jnp.arange(half).astype(F32) / half)
    angles = step.astype(F32) * freqs
    return jnp.concatenate([jnp.cos(angles), jnp.sin(angles)])


def place_embed(slots, width):
    quarter = D // 4
    omega = jnp.power(10000.0, -jnp.arange(quarter).astype(F32) / quarter)
    angle = jnp.arange(SIDE).astype(F32)[:, None] * omega
    table = jnp.concatenate([jnp.sin(angle), jnp.cos(angle)], axis=1)
    places = jnp.arange(SIDE)[None]
    row = ((slots // width)[:, None] == places).astype(F32)
    col = ((slots % width)[:, None] == places).astype(F32)
    return jnp.concatenate(
        [jnp.dot(row, table, precision=HIGH), jnp.dot(col, table, precision=HIGH)], axis=1
    )


def normalize(state):
    centered = state - jnp.mean(state, axis=-1, keepdims=True)
    spread = jnp.mean(centered * centered, axis=-1, keepdims=True)
    return centered * lax.rsqrt(spread + NORM_EPS)


def modulate(state, shift, scale):
    return normalize(state) * (1.0 + scale) + shift


def gelu_tanh(value):
    return jax.nn.gelu(value, approximate=True)


def contract_rows(left, right):
    return lax.dot_general(left, right, (((0,), (0,)), ((), ())), preferred_element_type=F32)


def contract_cols(left, right):
    return lax.dot_general(left, right, (((1,), (1,)), ((), ())), preferred_element_type=F32)


def size_of(axes):
    size = 1
    for axis in axes:
        size = size * lax.axis_size(axis)
    return size


def index_of(axes):
    index = 0
    for axis in axes:
        index = index * lax.axis_size(axis) + lax.axis_index(axis)
    return index


def from_others(pick, axes):
    size = size_of(axes)
    return [pick(0)] + [
        lax.ppermute(pick(k), axes, [(i, i ^ k) for i in range(size)]) for k in range(1, size)
    ]


def tree_sum(values):
    while len(values) > 1:
        values = [values[i] + values[i + 1] for i in range(0, len(values), 2)]
    return values[0]


def all_sum(value, groups=(("c",), ("y", "x"), ("z",))):
    for axes in groups:
        value = tree_sum(from_others(lambda k: value, axes))
    return value


def gather_rows(value, groups):
    for axes in groups:
        found = jnp.stack(from_others(lambda k: value, axes))
        size, me = size_of(axes), index_of(axes)
        bit = 1
        while bit < size:
            pairs = found.reshape((size // (2 * bit), 2, bit) + value.shape)
            found = jnp.where((me & bit) == 0, pairs, pairs[:, ::-1]).reshape(found.shape)
            bit *= 2
        value = found.reshape((-1,) + value.shape[1:])
    return value


def scatter_rows(value, axes):
    size, me = size_of(axes), index_of(axes)
    parts = value.reshape((size, -1) + value.shape[1:])
    return tree_sum(
        from_others(lambda k: lax.dynamic_index_in_dim(parts, me ^ k, 0, keepdims=False), axes)
    )


def columns_by_core(value):
    parts = value.reshape(value.shape[:-1] + (2, -1))
    c = lax.axis_index("c")
    keep = lax.dynamic_index_in_dim(parts, c, -2, keepdims=False)
    send = lax.dynamic_index_in_dim(parts, 1 - c, -2, keepdims=False)
    return keep + lax.ppermute(send, "c", SWAP)


def columns_of_cores(value):
    other = lax.ppermute(value, "c", SWAP)
    c = lax.axis_index("c")
    return jnp.where(
        c == 0, jnp.concatenate([value, other], -1), jnp.concatenate([other, value], -1)
    )


def own_sequence(values):
    x = lax.axis_index("x")
    send = lax.dynamic_index_in_dim(values, 1 - x, 0, keepdims=False)
    keep = lax.dynamic_index_in_dim(values, x, 0, keepdims=False)
    other = lax.ppermute(send, "x", SWAP)
    pair = jnp.where(x == 0, jnp.stack([keep, other]), jnp.stack([other, keep]))
    more = lax.ppermute(pair, "c", SWAP)
    both = jnp.where(
        lax.axis_index("c") == 0, jnp.stack([pair, more], 1), jnp.stack([more, pair], 1)
    )
    return both.transpose(2, 0, 1, 3).reshape(values.shape[1], -1)


def strips_of(tiles, is_mixer):
    count = tiles.shape[0] // 12
    plain = (
        tiles.reshape(count, 3, 4, BLK, BLK).transpose(0, 1, 3, 2, 4).reshape(count, STRIP, D)
    )
    turned = (
        tiles.reshape(count, 4, 3, BLK, BLK).transpose(0, 2, 4, 1, 3).reshape(count, STRIP, D)
    )
    return jnp.where(is_mixer, turned, plain)


def tiles_of(strips, is_mixer):
    count = strips.shape[0]
    plain = (
        strips.reshape(count, 3, BLK, 4, BLK).transpose(0, 1, 3, 2, 4).reshape(-1, BLK, BLK)
    )
    turned = (
        strips.reshape(count, 3, BLK, 4, BLK).transpose(0, 3, 1, 4, 2).reshape(-1, BLK, BLK)
    )
    return jnp.where(is_mixer, turned, plain)


def select_y(own, other):
    first = lax.axis_index("y") == 0
    return jnp.where(first, own, other), jnp.where(first, other, own)


HALF = STRIP // 2


class Overlap:
    def __init__(self):
        self.before = []
        self.source = None
        self.moves = []

    def feed(self, source):
        self.source = source
        self.advance(None)

    def advance(self, got):
        try:
            self.moves = self.source.send(got)
        except StopIteration:
            self.source = None
            self.moves = []

    def beside(self, work, *carry):
        values = [move[0] for move in self.moves]
        unused, values, carry = lax.optimization_barrier((self.before, values, carry))
        got = [lax.ppermute(value, move[1], move[2]) for value, move in zip(values, self.moves)]
        result = work(*carry)
        self.before = got
        if self.source is not None:
            self.advance(got)
        return result

    def alone(self, work, *carry):
        self.before, carry = lax.optimization_barrier((self.before, carry))
        result = work(*carry)
        self.before = [jax.tree.leaves(result), self.before]
        return result


def by_plane(options):
    z = lax.axis_index("z")
    chosen = None
    for place, value in options.items():
        chosen = value if chosen is None else jnp.where(z == place, value, chosen)
    return chosen


PARTS = [(0, 176), (176, 160), (336, 176), (512, 160)]
LATE = (672, 192)
HALVES = [(672, 96), (768, 96)]


def place():
    return [lax.axis_index(name) for name in ("z", "y", "x", "c")]


def meet(devices):
    barrier = pltpu.get_barrier_semaphore()
    z = lax.axis_index("z")
    amount = 2
    for key, device in devices.items():
        if key in ("up", "down"):
            there = (z < 3) if key == "up" else (z > 0)

            @pl.when(there)
            def signal(device=device):
                pl.semaphore_signal(barrier, 1, device_id=device, device_id_type=pl.DeviceIdType.MESH)

            amount = amount + there.astype(jnp.int32)
        else:
            pl.semaphore_signal(barrier, 1, device_id=device, device_id_type=pl.DeviceIdType.MESH)
    pl.semaphore_wait(barrier, amount)


def neighbours():
    z, y, x, c = place()
    return {
        "x": (z, y, 1 - x, c),
        "y": (z, 1 - y, x, c),
        "up": (jnp.minimum(z + 1, 3), y, x, c),
        "down": (jnp.maximum(z - 1, 0), y, x, c),
    }


def gather_kernel(strip_ref, out_ref, own_sem, send_z, recv_z, send_p, recv_p, send_c, recv_c):
    z, y, x, c = place()
    device = neighbours()
    meet(device)

    def region(far, plane, yi, rows):
        at = pl.multiple_of((2 * plane + yi) * STRIP + rows[0], 16)
        return out_ref.at[far, pl.ds(at, rows[1]), :]

    def copy(far, plane, yi, rows, key, send, recv):
        return pltpu.make_async_remote_copy(
            src_ref=region(far, plane, yi, rows),
            dst_ref=region(1 - far if key == "x" else far, plane, yi, rows),
            send_sem=send,
            recv_sem=recv,
            device_id=device[key],
            device_id_type=pl.DeviceIdType.MESH,
        )

    own = pltpu.make_async_copy(strip_ref, region(0, z, y, (0, STRIP)), own_sem)
    own.start()

    def valid(d):
        if d == 0:
            return None
        return (z >= d) if d > 0 else (z <= 3 + d)

    def run(condition, action):
        if condition is None:
            action()
        else:
            pl.when(condition)(action)

    def plane_copies(d, p, rows, first):
        second = "y" if first == "x" else "x"
        plane = z - d
        sems = [(send_p.at[d + 3, p, hop], recv_p.at[d + 3, p, hop]) for hop in range(3)]
        hop1 = copy(0, plane, y, rows, first, *sems[0])
        hop2 = copy(0, plane, y, rows, second, *sems[1])
        got = (1, y) if first == "x" else (0, 1 - y)
        hop3 = copy(got[0], plane, got[1], rows, second, *sems[2])
        return hop1, hop2, hop3

    def z_copy(d, p, key):
        index = d + 3
        nxt = index + 1 if key == "up" else index - 1
        slot = 0 if key == "up" else 1
        return copy(0, z - d, y, PARTS[p], key, send_z.at[index, p, slot], recv_z.at[nxt, p])

    def z_wait(d, p):
        key = "down" if d > 0 else "up"
        copy(0, z - d, y, PARTS[p], key, send_z.at[3, p, 0], recv_z.at[d + 3, p]).wait_recv()

    firsts = ["x", "y", "x", "y"]
    events = sorted(
        [(d, p) for d in range(-3, 4) for p in range(4)], key=lambda e: (abs(e[0]) + e[1], abs(e[0]))
    )
    lag = 16
    todo = []

    def forward(d, p):
        hop1, hop2, hop3 = plane_copies(d, p, PARTS[p], firsts[p])

        def action():
            hop1.wait_recv()
            hop3.start()

        run(valid(d), action)

    own.wait()
    for h in range(2):
        hop1, hop2, hop3 = plane_copies(0, 4 + h, HALVES[h], firsts[h])
        hop1.start()
        hop2.start()
    for number, (d, p) in enumerate(events):

        def action(d=d, p=p):
            if d != 0:
                z_wait(d, p)
            if d >= 0:
                run(z < 3, lambda: z_copy(d, p, "up").start())
            if d <= 0:
                run(z > 0, lambda: z_copy(d, p, "down").start())
            hop1, hop2, hop3 = plane_copies(d, p, PARTS[p], firsts[p])
            hop1.start()
            hop2.start()

        run(valid(d), action)
        if number == 3:
            for h in range(2):
                hop1, hop2, hop3 = plane_copies(0, 4 + h, HALVES[h], firsts[h])
                hop1.wait_recv()
                hop3.start()
        todo.append((d, p))
        if len(todo) > lag:
            forward(*todo.pop(0))

    def late(d, xi, yi, key):
        index = d + 3
        nxt = index + 1 if key == "up" else index - 1
        slot = 0 if key == "up" else 1
        k = 2 * xi + yi
        return copy(xi, z - d, yi, LATE, key, send_c.at[index, k, slot], recv_c.at[nxt, k])

    def late_wait(d, xi, yi):
        key = "down" if d > 0 else "up"
        k = 2 * xi + yi
        copy(xi, z - d, yi, LATE, key, send_c.at[3, 0, 0], recv_c.at[d + 3, k]).wait_recv()

    for h in range(2):
        unused, hop2, hop3 = plane_copies(0, 4 + h, HALVES[h], firsts[h])
        hop2.wait_recv()
        hop3.wait_recv()
    for distance in range(4):
        for xi in range(2):
            for yi in range(2):
                for d in ([0] if distance == 0 else [distance, -distance]):

                    def action(d=d, xi=xi, yi=yi):
                        if d != 0:
                            late_wait(d, xi, yi)
                        if d >= 0 and d < 3:
                            run(z < 3, lambda: late(d, xi, yi, "up").start())
                        if d <= 0 and d > -3:
                            run(z > 0, lambda: late(d, xi, yi, "down").start())

                    run(valid(d), action)
                if todo:
                    forward(*todo.pop(0))
    while todo:
        forward(*todo.pop(0))

    for d, p in events:

        def action(d=d, p=p):
            hop1, hop2, hop3 = plane_copies(d, p, PARTS[p], firsts[p])
            hop2.wait_recv()
            hop3.wait_recv()
            hop1.wait_send()
            hop2.wait_send()
            hop3.wait_send()
            if d >= 0:
                run(z < 3, lambda: z_copy(d, p, "up").wait_send())
            if d <= 0:
                run(z > 0, lambda: z_copy(d, p, "down").wait_send())

        run(valid(d), action)
    for h in range(2):
        hop1, hop2, hop3 = plane_copies(0, 4 + h, HALVES[h], firsts[h])
        hop1.wait_send()
        hop2.wait_send()
        hop3.wait_send()
    for d in range(-3, 4):
        for xi in range(2):
            for yi in range(2):

                def action(d=d, xi=xi, yi=yi):
                    if d >= 0 and d < 3:
                        run(z < 3, lambda: late(d, xi, yi, "up").wait_send())
                    if d <= 0 and d > -3:
                        run(z > 0, lambda: late(d, xi, yi, "down").wait_send())

                run(valid(d), action)


def gather_strips(strip):
    return pl.pallas_call(
        gather_kernel,
        out_shape=jax.ShapeDtypeStruct((2, 8 * STRIP, D), BF16),
        in_specs=[pl.BlockSpec(memory_space=pl.ANY)],
        out_specs=pl.BlockSpec(memory_space=pl.ANY),
        scratch_shapes=[
            pltpu.SemaphoreType.DMA,
            pltpu.SemaphoreType.DMA((7, 4, 2)),
            pltpu.SemaphoreType.DMA((7, 4)),
            pltpu.SemaphoreType.DMA((7, 6, 3)),
            pltpu.SemaphoreType.DMA((7, 6, 3)),
            pltpu.SemaphoreType.DMA((7, 4, 2)),
            pltpu.SemaphoreType.DMA((7, 4)),
        ],
        compiler_params=pltpu.CompilerParams(collective_id=1, has_side_effects=True),
        name="gather_strips",
    )(strip)


def gather_any(tiles, planes):
    whole = lax.all_gather(tiles, ("z", "y", "x"), axis=0, tiled=False)
    x = lax.axis_index("x")
    whole = whole.reshape((-1, 2) + tiles.shape)
    groups = []
    for place in (x, 1 - x):
        blocks = lax.dynamic_index_in_dim(whole, place, 1, keepdims=False)
        blocks = blocks.reshape(-1, BLK, BLK)
        groups.append(strips_of(blocks, (jnp.arange(8) % 4 == 0)[:, None, None]))
    for plane in range(4):
        planes[plane] = [(groups[i][2 * plane], groups[i][2 * plane + 1]) for i in range(2)]


def add_low(left, right):
    return (left.astype(F32) + right.astype(F32)).astype(BF16)


def line_moves(parts, plane, done):
    parts = list(parts)
    rights, lefts = plane, 3 - plane
    hops = max(rights, lefts)
    for step in range(hops + 1):
        moves, which = [], []
        for i in range(2):
            hop = step - i
            if 0 <= hop < hops:
                if hop < rights:
                    moves.append((parts[i], "z", [(hop, hop + 1)]))
                    which.append(i)
                if hop < lefts:
                    moves.append((parts[i], "z", [(3 - hop, 2 - hop)]))
                    which.append(i)
        got = yield moves
        for i, value in zip(which, got):
            parts[i] = add_low(parts[i], value)
    done[plane] = jnp.concatenate(parts)
    yield None


def reduce_strips(planes, done):
    y = lax.axis_index("y")
    lines = []

    def pick(pair, own):
        first = (y == 0) if own else (y == 1)
        return jnp.where(first, pair[0], pair[1])

    def everything(moves):
        whole = list(moves)
        spans = []
        for line in lines:
            spans.append((line, len(whole), len(whole) + len(line[1])))
            whole += line[1]
        return whole, spans

    def settle(got, spans):
        for line, begin, end in spans:
            line[1] = line[0].send(got[begin:end])
            if line[1] is None:
                lines.remove(line)

    for plane in (3, 2, 1, 0):
        grads = planes[plane]
        send_x = jnp.stack([part[:HALF] for part in grads[1]])
        lows = [[part[HALF:] for part in group] for group in grads]
        send_y = jnp.stack([pick(group, False) for group in lows])
        moves, spans = everything([(send_x, "x", SWAP), (send_y, "y", SWAP)])
        got = yield moves
        settle(got, spans)
        upper = [add_low(grads[0][i][:HALF], got[0][i]) for i in range(2)]
        lower = [add_low(pick(lows[i], True), got[1][i]) for i in range(2)]
        moves, spans = everything([(pick(upper, False), "y", SWAP), (lower[1], "x", SWAP)])
        got = yield moves
        settle(got, spans)
        parts = [add_low(pick(upper, True), got[0]), add_low(lower[0], got[1])]
        line = line_moves(parts, plane, done)
        lines.append([line, next(line)])
        if plane % 2 == 1:
            moves, spans = everything([])
            got = yield moves
            settle(got, spans)
    while lines:
        moves, spans = everything([])
        got = yield moves
        settle(got, spans)


def reduce_any(planes, count):
    x = lax.axis_index("x")
    groups = []
    for place in range(2):
        chosen = [
            jnp.where(x == place, planes[plane][0][y], planes[plane][1][y])
            for plane in range(4)
            for y in range(2)
        ]
        blocks = tiles_of(jnp.stack(chosen), jnp.zeros((), bool)).reshape(8, 12, BLK, BLK)
        turned = tiles_of(jnp.stack(chosen), jnp.ones((), bool)).reshape(8, 12, BLK, BLK)
        mixer = (jnp.arange(8) % 4 == 0)[:, None, None, None]
        groups.append(jnp.where(mixer, turned, blocks).reshape(-1, count, BLK, BLK))
    whole = jnp.stack(groups, axis=1).reshape(-1, BLK, BLK)
    return lax.psum_scatter(whole, ("z", "y", "x"), scatter_dimension=0, tiled=True)


def pad_to(value, step):
    return -(-value // step) * step


def piece_at(first, base, width, height):
    skip = jnp.minimum(jnp.maximum(first - base, 0) // width, height)
    return skip, base + skip * width - first + FRONT


def split_dot(left, right, dims):
    return lax.dot_general(
        left, right, (dims, ((), ())), precision=HIGH, preferred_element_type=F32
    )


class Flat:
    def __init__(self, length):
        start = index_of(("z", "y", "x", "c")) * length
        self.length = length
        self.where = jnp.stack([start // LANE, start % LANE]).astype(jnp.int32)
        self.packed = pad_to(-(-length // LANE), 8)
        self.rows = self.packed + 8
        self.total = FRONT + self.rows + pad_to(self.rows + 3 * ROW_ADA * 8, 8)

    def count(self, width, height):
        return pad_to(min(height, self.rows // width + 2), 8)

    def call(self, body, outs, operands, scratch=(), name="flat"):
        def kernel(where, *refs):
            body(where[0], where[1], *refs)

        amount = len(operands)
        return pl.pallas_call(
            kernel,
            out_shape=outs,
            in_specs=[pl.BlockSpec(memory_space=pltpu.SMEM)]
            + [pl.BlockSpec(memory_space=pltpu.VMEM)] * amount,
            out_specs=jax.tree.map(lambda v: pl.BlockSpec(memory_space=pltpu.VMEM), outs),
            scratch_shapes=list(scratch),
            compiler_params=pltpu.CompilerParams(vmem_limit_bytes=52 * 1024 * 1024),
            name=name,
        )(self.where, *operands)

    def when_here(self, first, piece, action):
        base, width, height = piece
        skip, at = piece_at(first, base, width, height)

        @pl.when((skip < height) & (at < FRONT + self.rows))
        def run():
            action(skip, at)

    def padded(self, factor, width):
        count = self.count(width, factor.shape[1])
        return jnp.pad(factor.astype(F32).T, ((0, count), (0, 0)))

    def align(self, shard):
        flat = jnp.pad(shard, (0, self.packed * LANE - self.length)).reshape(self.packed, LANE)

        def body(first, skew, flat_ref, held_ref):
            held_ref[:FRONT] = jnp.zeros((FRONT, LANE), F32)
            values = flat_ref[...].astype(BF16).astype(F32)
            turned = pltpu.roll(values, skew, 1)
            lanes = lax.broadcasted_iota(jnp.int32, (self.packed, LANE), 1)
            empty = jnp.zeros((8, LANE), F32)
            here = jnp.where(lanes >= skew, turned, 0.0)
            carry = jnp.where(lanes >= skew, 0.0, turned)
            held_ref[FRONT : FRONT + self.packed] = here
            held_ref[FRONT + self.packed :] = jnp.zeros(
                (self.total - FRONT - self.packed, LANE), F32
            )
            held_ref[FRONT + 1 : FRONT + 1 + self.packed] += carry

        return self.call(
            body, jax.ShapeDtypeStruct((self.total, LANE), F32), [flat], name="align"
        )

    def take(self, held, pieces):
        amount = sum(height for base, height in pieces)
        size = pad_to(2 * amount, 8)

        def body(first, skew, held_ref, out_ref):
            out_ref[...] = jnp.zeros_like(out_ref)
            put = 0
            for base, height in pieces:

                def action(skip, at, put=put, height=height):
                    block = held_ref[pl.ds(at, height), :]
                    index = lax.broadcasted_iota(jnp.int32, (height, LANE), 0)
                    out_ref[pl.ds(put + skip, height), :] = jnp.where(
                        index < height - skip, block, 0.0
                    )

                self.when_here(first, (base, 1, height), action)
                put += height

        out = self.call(body, jax.ShapeDtypeStruct((size, LANE), F32), [held], name="take")
        return out[:amount]

    def product(self, held, factors, pieces, exact, join):
        operands = [self.padded(f, piece[1]) for f, piece in zip(factors, pieces)]
        number = factors[0].shape[0]
        wide = [piece[1] * LANE for piece in pieces]
        out = jax.ShapeDtypeStruct((number, wide[0] if join else sum(wide)), F32)

        def body(first, skew, held_ref, *refs):
            out_ref = refs[-1]
            out_ref[...] = jnp.zeros_like(out_ref)
            put = 0
            for piece, factor_ref in zip(pieces, refs[:-1]):
                base, width, height = piece
                count = self.count(width, height)

                def action(skip, at, width=width, count=count, factor_ref=factor_ref, put=put):
                    near = factor_ref[pl.ds(skip, count), :]
                    near = near if exact else near.astype(BF16)
                    for u in range(width):
                        block = held_ref[pl.ds(at + u, count, stride=width), :]
                        if exact:
                            value = split_dot(near, block, ((0,), (0,)))
                        else:
                            value = contract_rows(near, block.astype(BF16))
                        out_ref[:, put + u * LANE : put + (u + 1) * LANE] += value

                self.when_here(first, piece, action)
                put = put if join else put + width * LANE

        return self.call(body, out, [held] + operands, name="product")

    def back_product(self, held, grads, pieces):
        number, height = grads[0].shape[0], pieces[0][2]
        most = max(self.count(piece[1], height) for piece in pieces)

        def body(first, skew, held_ref, *refs):
            out_ref = refs[-1]
            out_ref[...] = jnp.zeros_like(out_ref)
            for piece, grad_ref in zip(pieces, refs[:-1]):
                width = piece[1]
                count = self.count(width, height)

                def action(skip, at, width=width, count=count, grad_ref=grad_ref):
                    value = jnp.zeros((count, number), F32)
                    for u in range(width):
                        block = held_ref[pl.ds(at + u, count, stride=width), :]
                        grad = grad_ref[:, u * LANE : (u + 1) * LANE]
                        value = value + split_dot(block, grad, ((1,), (1,)))
                    out_ref[pl.ds(skip, count), :] += value

                self.when_here(first, piece, action)

        out = self.call(
            body,
            jax.ShapeDtypeStruct((height + most, number), F32),
            [held] + list(grads),
            name="back_product",
        )
        return out[:height].T

    def gradient(self, parts):
        operands, plan = ([], [])
        for part in parts:
            if len(part) == 2:
                base, values = part
                height = values.shape[0]
                operands.append(jnp.pad(values, ((0, height), (0, 0))))
                plan.append((base, 1, height, len(operands) - 1, None))
            else:
                base, width, left, right = part
                operands += [self.padded(left, width), right]
                plan.append((base, width, left.shape[1], len(operands) - 2, len(operands) - 1))

        def body(first, skew, *refs):
            grad_ref, square_ref, rows_ref = refs[-3:]
            for base, width, height, one, two in plan:

                def vector(skip, at, height=height, one=one):
                    rows_ref[pl.ds(at, height), :] = refs[one][pl.ds(skip, height), :]

                def outer(skip, at, width=width, height=height, one=one, two=two):
                    count = self.count(width, height)
                    near = refs[one][pl.ds(skip, count), :]
                    for u in range(width):
                        grad = refs[two][:, u * LANE : (u + 1) * LANE]
                        rows_ref[pl.ds(at + u, count, stride=width), :] = split_dot(
                            near, grad, ((1,), (0,))
                        )

                self.when_here(first, (base, width, height), vector if two is None else outer)
            lanes = lax.broadcasted_iota(jnp.int32, (self.packed, LANE), 1)
            index = lax.broadcasted_iota(jnp.int32, (self.packed, LANE), 0)
            back = (LANE - skew) % LANE
            here = pltpu.roll(rows_ref[FRONT : FRONT + self.packed], back, 1)
            after = pltpu.roll(rows_ref[FRONT + 1 : FRONT + 1 + self.packed], back, 1)
            value = jnp.where(lanes < LANE - skew, here, after)
            value = jnp.where(index * LANE + lanes < self.length, value, 0.0)
            grad_ref[...] = value
            square_ref[...] = jnp.sum(
                jnp.sum(value * value, axis=0, keepdims=True), axis=1, keepdims=True
            )

        grad, square = self.call(
            body,
            (
                jax.ShapeDtypeStruct((self.packed, LANE), F32),
                jax.ShapeDtypeStruct((1, 1), F32),
            ),
            operands,
            [pltpu.VMEM((self.total, LANE), F32)],
            name="flat_gradient",
        )
        return grad.reshape(-1)[: self.length], square[0, 0]


def dot(a, b):
    return jnp.dot(a, b, preferred_element_type=F32)


def attend_kernel(block, mixed_ref, bias_ref, out_ref, log_ref, keys, values, query):
    rows = mixed_ref.shape[1]
    wide = mixed_ref[...].astype(F32)
    extra = jnp.concatenate([bias_ref[...], jnp.zeros((7, rows), F32)], axis=0)
    ones = jnp.concatenate([jnp.ones((1, rows), F32), jnp.zeros((7, rows), F32)], axis=0)
    for h in range(HEADS_HERE):
        q = wide[h * HD : (h + 1) * HD]
        k = wide[WIDE + h * HD : WIDE + (h + 1) * HD]
        v = wide[2 * WIDE + h * HD : 2 * WIDE + (h + 1) * HD]
        query[h] = jnp.concatenate([q, ones], axis=0).astype(BF16)
        keys[h] = jnp.concatenate([k, extra], axis=0).T.astype(BF16)
        values[h] = jnp.concatenate([v, jnp.zeros((8, rows), F32)], axis=0).astype(BF16)

    def step(i, unused):
        at = pl.multiple_of(i * block, block)
        outs = []
        logs = []
        for h in range(HEADS_HERE):
            raw = dot(keys[h], query[h, :, pl.ds(at, block)])
            top = jnp.max(raw, axis=0, keepdims=True)
            expo = jnp.exp2((raw - top) * SC2)
            total = jnp.sum(expo, axis=0, keepdims=True)
            out = dot(values[h], expo.astype(BF16))[:HD]
            outs.append(out / total)
            logs.append(top * SC2 + jnp.log2(total))
        out_ref[:, pl.ds(at, block)] = jnp.concatenate(outs, axis=0).astype(BF16)
        log_ref[:, pl.ds(at, block)] = jnp.concatenate(logs + logs, axis=0)
        return unused

    lax.fori_loop(0, rows // block, step, 0)


def attend(mixed, bias, block=512):
    rows = mixed.shape[1]
    return pl.pallas_call(
        functools.partial(attend_kernel, block),
        out_shape=(
            jax.ShapeDtypeStruct((WIDE, rows), BF16),
            jax.ShapeDtypeStruct((8, rows), F32),
        ),
        scratch_shapes=[
            pltpu.VMEM((HEADS_HERE, rows, 80), BF16),
            pltpu.VMEM((HEADS_HERE, 80, rows), BF16),
            pltpu.VMEM((HEADS_HERE, 80, rows), BF16),
        ],
        compiler_params=pltpu.CompilerParams(vmem_limit_bytes=48 * 1024 * 1024),
        cost_estimate=pl.CostEstimate(
            flops=4 * HEADS_HERE * rows * rows * HD,
            bytes_accessed=8 * WIDE * rows,
            transcendentals=HEADS_HERE * rows * rows,
        ),
        name="attend",
    )(mixed, bias)


def attend_back_kernel(
    block, mixed_ref, bias_ref, out_ref, log_ref, grad_ref, result_ref,
    keys, values, query, keys_t, query_t, grads, grads_t, sum_k, sum_v, grad_q, delta,
):
    rows = mixed_ref.shape[1]
    wide = mixed_ref[...].astype(F32)
    gwide = grad_ref[...].astype(F32)
    owide = out_ref[...].astype(F32)
    extra = jnp.concatenate([bias_ref[...], jnp.zeros((7, rows), F32)], axis=0)
    ones = jnp.concatenate([jnp.ones((1, rows), F32), jnp.zeros((7, rows), F32)], axis=0)
    none = jnp.zeros((8, rows), F32)
    deltas = []
    for h in range(HEADS_HERE):
        q = wide[h * HD : (h + 1) * HD]
        k = wide[WIDE + h * HD : WIDE + (h + 1) * HD]
        v = wide[2 * WIDE + h * HD : 2 * WIDE + (h + 1) * HD]
        g = gwide[h * HD : (h + 1) * HD]
        o = owide[h * HD : (h + 1) * HD]
        query[h] = jnp.concatenate([q, ones], axis=0).astype(BF16)
        query_t[h] = jnp.concatenate([q, none], axis=0).T.astype(BF16)
        keys[h] = jnp.concatenate([k, extra], axis=0).T.astype(BF16)
        keys_t[h] = jnp.concatenate([k, none], axis=0).astype(BF16)
        values[h] = jnp.concatenate([v, none], axis=0).T.astype(BF16)
        grads[h] = jnp.concatenate([g, none], axis=0).astype(BF16)
        grads_t[h] = jnp.concatenate([g, none], axis=0).T.astype(BF16)
        deltas.append(jnp.sum(g * o, axis=0, keepdims=True))
    delta[...] = jnp.concatenate(deltas + deltas, axis=0)
    sum_k[...] = jnp.zeros_like(sum_k)
    sum_v[...] = jnp.zeros_like(sum_v)

    def step(i, unused):
        at = pl.multiple_of(i * block, block)
        here = pl.ds(at, block)
        for h in range(HEADS_HERE):
            raw = dot(keys[h], query[h, :, here])
            probs = jnp.exp2(raw * SC2 - log_ref[h : h + 1, here])
            grad_probs = dot(values[h], grads[h, :, here])
            grad_raw = (probs * (grad_probs - delta[h : h + 1, here])).astype(BF16)
            sum_v[h] += dot(probs.astype(BF16), grads_t[h, here, :])
            sum_k[h] += dot(grad_raw, query_t[h, here, :])
            grad_q[h, :, here] = dot(keys_t[h], grad_raw)
        return unused

    lax.fori_loop(0, rows // block, step, 0)
    parts = [grad_q[h][:HD] * SCALE for h in range(HEADS_HERE)]
    parts += [(sum_k[h].T)[:HD] * SCALE for h in range(HEADS_HERE)]
    parts += [(sum_v[h].T)[:HD] for h in range(HEADS_HERE)]
    result_ref[...] = jnp.concatenate(parts, axis=0).astype(BF16)


def attend_back(mixed, bias, out, logs, grad, block=512):
    rows = mixed.shape[1]
    n = HEADS_HERE
    return pl.pallas_call(
        functools.partial(attend_back_kernel, block),
        out_shape=jax.ShapeDtypeStruct((3 * WIDE, rows), BF16),
        scratch_shapes=[
            pltpu.VMEM((n, rows, 80), BF16),
            pltpu.VMEM((n, rows, 80), BF16),
            pltpu.VMEM((n, 80, rows), BF16),
            pltpu.VMEM((n, 80, rows), BF16),
            pltpu.VMEM((n, rows, 80), BF16),
            pltpu.VMEM((n, 80, rows), BF16),
            pltpu.VMEM((n, rows, 80), BF16),
            pltpu.VMEM((n, rows, 80), F32),
            pltpu.VMEM((n, rows, 80), F32),
            pltpu.VMEM((n, 80, rows), F32),
            pltpu.VMEM((8, rows), F32),
        ],
        compiler_params=pltpu.CompilerParams(vmem_limit_bytes=48 * 1024 * 1024),
        cost_estimate=pl.CostEstimate(
            flops=10 * n * rows * rows * HD,
            bytes_accessed=18 * WIDE * rows,
            transcendentals=n * rows * rows,
        ),
        name="attend_back",
    )(mixed, bias, out, logs, grad)


def join_cores(partial):
    low = partial.astype(BF16)
    return low.astype(F32) + lax.ppermute(low, "c", SWAP).astype(F32)


def rank_columns(vector, groups, rank, ranks):
    return lax.dynamic_index_in_dim(
        vector.reshape(groups, ranks, -1), rank, 1, keepdims=False
    ).reshape(-1)


def spread_columns(grads, groups, ranks_here, ranks):
    total = 0.0
    for grad, rank in zip(grads, ranks_here):
        width = grad.shape[0] // groups
        select = (jnp.arange(ranks) == rank).astype(F32)
        total = total + (grad.reshape(groups, 1, width) * select[None, :, None]).reshape(-1)
    return total


class Layer:
    def __init__(self, modulation, biases, ranks_here, ranks, keymask):
        pieces = jnp.split(modulation, 6)
        self.shift_a, self.scale_a, self.gate_a = pieces[:3]
        self.shift_b, self.scale_b, self.gate_b = pieces[3:]
        self.qkv_b, self.proj_b, self.up_b, self.down_b = biases
        self.ranks_here, self.ranks, self.keymask = ranks_here, ranks, keymask

    def take_whole(self, whole, index):
        at = 4 * STRIP * index
        rows = [at, at + STRIP, at + 4 * BLK, at + 8 * BLK, at + 12 * BLK]
        parts = [[whole[i, rows[n] : rows[n + 1]] for i in range(2)] for n in range(4)]
        self.mixer, self.proj, self.up_w, self.down_w = parts

    def take_planes(self, upper, lower):
        self.mixer = [upper[i][0] for i in range(2)]
        self.proj = [upper[i][1][:BLK] for i in range(2)]
        self.up_w = [jnp.concatenate([upper[i][1][BLK:], lower[i][0][: 2 * BLK]]) for i in range(2)]
        self.down_w = [jnp.concatenate([lower[i][0][2 * BLK :], lower[i][1]]) for i in range(2)]

    def mix_one(self, i, normed):
        bias = rank_columns(self.qkv_b, 3, self.ranks_here[i], self.ranks)
        return (contract_cols(self.mixer[i], normed) + bias[:, None]).astype(BF16)

    def mix_first(self, state):
        self.state = state
        normed = modulate(state, self.shift_a, self.scale_a).astype(BF16)
        return normed, self.mix_one(0, normed)

    def mix_second(self, normed, mixed):
        self.normed_a = normed
        out, logs = attend(mixed, self.keymask)
        self.mixed, self.out, self.logs = [mixed], [out], [logs]
        return self.mix_one(1, normed), out

    def attend_rest(self, mixed, out):
        more, logs = attend(mixed, self.keymask)
        self.mixed.append(mixed)
        self.out.append(more)
        self.logs.append(logs)
        return contract_rows(out, self.proj[0]) + contract_rows(more, self.proj[1])

    def join_attend(self, partial):
        self.attn = join_cores(partial) + self.proj_b
        return self.state + self.gate_a * self.attn

    def widen_one(self, i, normed):
        bias = rank_columns(self.up_b, 1, self.ranks_here[i], self.ranks)
        pre = jnp.dot(normed, self.up_w[i], preferred_element_type=F32) + bias
        return pre, gelu_tanh(pre).astype(BF16)

    def widen_first(self, middle):
        self.middle = middle
        normed = modulate(middle, self.shift_b, self.scale_b).astype(BF16)
        return normed, self.widen_one(0, normed)

    def widen_second(self, normed, first):
        self.normed_b = normed
        return first, self.widen_one(1, normed)

    def narrow(self, first, second):
        self.pre = [first[0], second[0]]
        self.act = [first[1], second[1]]
        partial = 0.0
        for mat, one in zip(self.down_w, self.act):
            partial = partial + jnp.dot(one, mat, preferred_element_type=F32)
        self.mlp = join_cores(partial) + self.down_b
        return self.middle + self.gate_b * self.mlp

    def back_narrow(self, grad_out):
        self.grad_out = grad_out
        self.grad_gate_b = jnp.sum(grad_out * self.mlp, axis=0)
        grad_mlp = self.gate_b * grad_out
        self.grad_down_b = jnp.sum(grad_mlp, axis=0)
        grad_mlp = grad_mlp.astype(BF16)
        self.grad_down, grad_pre = ([], [])
        for i in range(2):
            self.grad_down.append(contract_rows(self.act[i], grad_mlp).astype(BF16))
            grad_act = contract_cols(grad_mlp, self.down_w[i])
            unused, gelu_pull = jax.vjp(gelu_tanh, self.pre[i])
            grad_pre.append(gelu_pull(grad_act)[0].astype(BF16))
        return grad_pre

    def back_widen(self, grad_pre, planes, index):
        self.grad_up, self.grad_up_b = ([], [])
        partial = 0.0
        for i in range(2):
            self.grad_up_b.append(jnp.sum(grad_pre[i].astype(F32), axis=0))
            self.grad_up.append(contract_rows(self.normed_b, grad_pre[i]).astype(BF16))
            partial = partial + contract_cols(grad_pre[i], self.up_w[i])
        unused, pull_b = jax.vjp(modulate, self.middle, self.shift_b, self.scale_b)
        grad_inner, self.grad_shift_b, self.grad_scale_b = pull_b(join_cores(partial))
        split = 2 * BLK
        planes[2 * index + 1] = [
            (
                jnp.concatenate([self.grad_up[i][split:], self.grad_down[i][:BLK]]),
                self.grad_down[i][BLK:],
            )
            for i in range(2)
        ]
        return self.grad_out + grad_inner

    def back_one(self, i):
        self.grad_proj.append(
            jnp.dot(self.out[i], self.grad_attn, preferred_element_type=F32).astype(BF16)
        )
        grad_attended = contract_cols(self.proj[i], self.grad_attn).astype(BF16)
        return attend_back(self.mixed[i], self.keymask, self.out[i], self.logs[i], grad_attended)

    def back_attend(self, grad_middle):
        self.grad_middle = grad_middle
        self.grad_gate_a = jnp.sum(grad_middle * self.attn, axis=0)
        grad_attn = self.gate_a * grad_middle
        self.grad_proj_b = jnp.sum(grad_attn, axis=0)
        self.grad_attn = grad_attn.astype(BF16)
        self.grad_proj = []
        return self.back_one(0), self.grad_attn

    def back_rest(self, grad_mixed, grad_attn):
        self.grad_attn = grad_attn
        return grad_mixed, self.back_one(1)

    def back_mix(self, grad_mixed):
        self.grad_mixer, self.grad_qkv_b = ([], [])
        for i in range(2):
            self.grad_qkv_b.append(jnp.sum(grad_mixed[i].astype(F32), axis=1))
            self.grad_mixer.append(
                jnp.dot(grad_mixed[i], self.normed_a, preferred_element_type=F32).astype(BF16)
            )
        return grad_mixed

    def back_join(self, grad_mixed, planes, index):
        grad_mixer, grad_qkv_b = self.grad_mixer, self.grad_qkv_b
        partial = 0.0
        for i in range(2):
            partial = partial + contract_rows(grad_mixed[i], self.mixer[i])
        unused, pull_a = jax.vjp(modulate, self.state, self.shift_a, self.scale_a)
        grad_state, grad_shift_a, grad_scale_a = pull_a(join_cores(partial))
        self.grad_mod = jnp.concatenate(
            [
                grad_shift_a,
                grad_scale_a,
                self.grad_gate_a,
                self.grad_shift_b,
                self.grad_scale_b,
                self.grad_gate_b,
            ]
        )
        once = jnp.where(lax.axis_index("c") == 0, 1.0, 0.0)
        self.grad_bias = jnp.concatenate(
            [
                spread_columns(grad_qkv_b, 3, self.ranks_here, self.ranks),
                self.grad_proj_b * once,
                spread_columns(self.grad_up_b, 1, self.ranks_here, self.ranks),
                self.grad_down_b * once,
            ]
        )
        split = 2 * BLK
        planes[2 * index] = [
            (
                grad_mixer[i],
                jnp.concatenate([self.grad_proj[i], self.grad_up[i][:split]]),
            )
            for i in range(2)
        ]
        return self.grad_middle + grad_state


def adamw(grad, moment, second, master):
    new_moment = ADAM_ONE * moment + (1.0 - ADAM_ONE) * grad
    new_second = ADAM_TWO * second + (1.0 - ADAM_TWO) * grad * grad
    fixed_moment = new_moment / (1.0 - ADAM_ONE**STEP_COUNT)
    fixed_second = new_second / (1.0 - ADAM_TWO**STEP_COUNT)
    new_master = master - ADAM_RATE * (
        fixed_moment / (jnp.sqrt(fixed_second) + ADAM_EPS) + ADAM_DECAY * master
    )
    return (new_moment, new_second, new_master)


def halves_dot(left, right, dims):
    left_high, right_high = left.astype(BF16), right.astype(BF16)
    left_low = (left - left_high.astype(F32)).astype(BF16)
    right_low = (right - right_high.astype(F32)).astype(BF16)

    def product(one, two):
        return lax.dot_general(one, two, (dims, ((), ())), preferred_element_type=F32)

    return product(left_high, right_high) + (
        product(left_high, right_low) + product(left_low, right_high)
    )


def shampoo_kernel(
    factor, grad, moment, left, right, left_inv, right_inv, master, *outs
):
    new_moment, new_left, new_right, new_master = outs
    clipped = grad[...].astype(F32) * factor[0]
    rows, columns = ((1,), (1,)), ((0,), (0,))
    new_left[...] = SHAMPOO_TWO * left[...] + (1.0 - SHAMPOO_TWO) * halves_dot(
        clipped, clipped, rows
    )
    new_right[...] = SHAMPOO_TWO * right[...] + (1.0 - SHAMPOO_TWO) * halves_dot(
        clipped, clipped, columns
    )
    mixed = SHAMPOO_ONE * moment[...] + (1.0 - SHAMPOO_ONE) * clipped
    new_moment[...] = mixed
    halfway = halves_dot(left_inv[...], mixed, ((1,), (0,)))
    direction = halves_dot(halfway, right_inv[...], ((1,), (0,)))
    new_master[...] = master[...] - SHAMPOO_RATE * (direction + SHAMPOO_DECAY * master[...])


def shampoo(factor, grad, moment, left, right, left_inv, right_inv, master):
    block = pl.BlockSpec((None, BLK, BLK), lambda i: (i, 0, 0))
    shape = jax.ShapeDtypeStruct(moment.shape, F32)
    return pl.pallas_call(
        shampoo_kernel,
        grid=(moment.shape[0],),
        out_shape=[shape] * 4,
        in_specs=[pl.BlockSpec(memory_space=pltpu.SMEM)] + [block] * 7,
        out_specs=[block] * 4,
        compiler_params=pltpu.CompilerParams(vmem_limit_bytes=48 * 1024 * 1024),
        name="shampoo",
    )(factor.reshape(1), grad, moment, left, right, left_inv, right_inv, master)


def local(
    latents,
    noise,
    timesteps,
    labels,
    grid,
    flat_master,
    flat_moment,
    flat_second,
    tile_master,
    tile_moment,
    tile_left,
    tile_right,
    left_root,
    right_root,
):
    x, y, z, c = [lax.axis_index(name) for name in ("x", "y", "z", "c")]
    groups = lax.axis_size("z") * lax.axis_size("y")
    ranks = lax.axis_size("x") * lax.axis_size("c")
    count_tiles = tile_master.shape[1]
    simple = lax.axis_size("y") == 2 and lax.axis_size("z") == 4 and count_tiles == 12
    ranks_here = [2 * x + c, 2 * (1 - x) + c]
    number = (z * lax.axis_size("y") + y) * 2 + x

    owner = z * lax.axis_size("y") + y
    is_mixer = owner % 4 == 0
    overlap = Overlap()
    planes = {}
    if simple:
        strip = strips_of(tile_master[0].astype(BF16), is_mixer)[0]
    else:
        gather_any(tile_master[0].astype(BF16), planes)
    flat = Flat(flat_master.shape[0])

    info = jnp.concatenate([timesteps[:, 0], labels[:, 0], grid[:, 0, 0], grid[:, 1, 0]])
    info = gather_rows(info.reshape(1, 4, MB), [("z", "y")])
    info = info.transpose(1, 0, 2).reshape(4, groups * MB)
    patches, target = own_sequence(latents), own_sequence(noise)
    held = flat.align(flat_master)
    overlap.before = [info, patches, target]
    count = jnp.sum((info[2] * info[3]).astype(F32))
    height = lax.dynamic_index_in_dim(info[2], number, 0, keepdims=False)
    width = lax.dynamic_index_in_dim(info[3], number, 0, keepdims=False)
    rows = patches.shape[1]
    slots = jnp.arange(rows)
    valid = slots < height * width
    keymask = jnp.where(valid, 0.0, -1e30).astype(F32)[None]

    freq = jax.vmap(time_freq)(info[0])
    onehot = (jnp.arange(CLASSES)[None, :] == info[1][:, None]).astype(F32)

    stem_axes = (("c",), ("y", "x"), ("z",))
    if BASE_TABLE * LANE <= ranks * flat.length:
        stem_axes = (("x", "c"),)
    w1, w2 = (BASE_W1, ROW_D, FREQ), (BASE_W2, ROW_D, D)
    table = (BASE_TABLE, ROW_D, CLASSES)
    final = (BASE_FINAL, ROW_FINAL, D)
    adas = [(BASE_LAYER + l * LAYER_ROWS, ROW_ADA, D) for l in range(LAYERS)]

    def small_work(held):
        vectors = [(0, ROW_STEM), (BASE_B1, ROW_D), (BASE_B2, ROW_D)]
        vectors += [(BASE_LAYER + l * LAYER_ROWS + D * ROW_ADA, ROW_BIAS) for l in range(LAYERS)]
        small = flat.take(held, vectors + [(BASE_TAIL, ROW_TAIL)]).astype(BF16)
        first = all_sum(small[ROW_STEM : ROW_STEM + ROW_D], stem_axes)
        hidden_pre = all_sum(flat.product(held, [freq], [w1], True, True), stem_axes)
        hidden_pre = hidden_pre + first.astype(F32).reshape(-1)
        hidden = jax.nn.silu(hidden_pre)
        cond = all_sum(
            flat.product(held, [hidden, onehot], [w2, table], True, True), (("c",), ("y", "x"))
        )
        return all_sum(small, (("c",), ("y", "x"))), hidden_pre, hidden, cond, held

    small, hidden_pre, hidden, cond, held = overlap.beside(small_work, held)
    small, cond = overlap.alone(
        lambda *v: [all_sum(one, (("z",),)) for one in v], small, cond
    )
    small = small.astype(F32)
    pieces = []
    at = 0
    for amount in [ROW_STEM, ROW_D, ROW_D] + [ROW_BIAS] * LAYERS + [ROW_TAIL]:
        pieces.append(small[at : at + amount].reshape(-1))
        at = at + amount
    stem, unused, time_b2 = pieces[:3]
    tail = pieces[-1]
    patch_w, patch_b = stem[: PATCH * D].reshape(PATCH, D), stem[PATCH * D :]
    final_b, head_w = tail[: 2 * D], tail[2 * D :].reshape(D, PATCH).astype(BF16)
    biases, ada_bs = ([], [])
    for layer in range(LAYERS):
        vector = pieces[3 + layer]
        ada_bs.append(vector[: 6 * D])
        biases.append(jnp.split(vector[6 * D :], [3 * D, 4 * D, 8 * D]))

    def mod_work(cond, held, small):
        cond = cond + small[ROW_STEM + ROW_D : ROW_STEM + 2 * ROW_D].reshape(-1)
        cond_s = jax.nn.silu(cond).astype(BF16)
        mods = flat.product(held, [cond_s] * 3, adas + [final], False, False)
        return cond, cond_s, columns_by_core(mods)

    cond, cond_s, mods = overlap.beside(mod_work, cond, held, small)
    mods = overlap.alone(lambda v: scatter_rows(v, ("z",)), mods)

    def stem_work(patches, mods):
        mods = columns_of_cores(scatter_rows(mods, ("y", "x")))[0]
        state = contract_rows(patches, patch_w.astype(BF16)) + patch_b + place_embed(slots, width)
        return state, mods

    state, mods = overlap.beside(stem_work, patches, mods)
    if simple:
        strip, state, mods = lax.optimization_barrier((strip, state, mods))
        whole = gather_strips(strip)
        state, whole = lax.optimization_barrier((state, whole))
    final_mod = mods[LAYERS * 6 * D :] + final_b
    layers = [
        Layer(mods[l * 6 * D : (l + 1) * 6 * D] + ada_bs[l], biases[l], ranks_here, ranks, keymask)
        for l in range(LAYERS)
    ]
    for index, layer in enumerate(layers):
        if simple:
            layer.take_whole(whole, index)
        else:
            layer.take_planes(planes[2 * index], planes[2 * index + 1])
        values = overlap.beside(layer.mix_first, state)
        values = overlap.beside(layer.mix_second, *values)
        values = overlap.beside(layer.attend_rest, *values)
        middle = overlap.beside(layer.join_attend, values)
        values = overlap.beside(layer.widen_first, middle)
        values = overlap.beside(layer.widen_second, *values)
        state = overlap.beside(layer.narrow, *values)
    shift_f, scale_f = jnp.split(final_mod, 2)
    normed_f = modulate(state, shift_f, scale_f).astype(BF16)
    predicted = jnp.dot(normed_f, head_w, preferred_element_type=F32)
    error = predicted - target.T
    loss_part = jnp.sum(jnp.where(valid[:, None], error * error, 0.0))
    grad_pred = jnp.where(valid[:, None], 2.0 * error / (PATCH * count), 0.0).astype(BF16)

    grad_head = contract_rows(normed_f, grad_pred)
    grad_normed_f = contract_cols(grad_pred, head_w)
    unused, pull_f = jax.vjp(modulate, state, shift_f, scale_f)
    grad_state, grad_shift_f, grad_scale_f = pull_f(grad_normed_f)
    grad_final = jnp.concatenate([grad_shift_f, grad_scale_f])
    grad_planes = {}
    done = {}
    for index in reversed(range(LAYERS)):
        layer = layers[index]
        grad_pre = overlap.beside(layer.back_narrow, grad_state)
        grad_middle = overlap.beside(
            lambda *v: layer.back_widen(v, grad_planes, index), *grad_pre
        )
        if simple and index == LAYERS - 1:
            overlap.feed(reduce_strips(grad_planes, done))
        grad_mixed = overlap.beside(layer.back_attend, grad_middle)
        grad_mixed = overlap.beside(layer.back_rest, *grad_mixed)
        grad_state = overlap.beside(
            lambda *v: layer.back_join(layer.back_mix(v), grad_planes, index), *grad_mixed
        )

    def factor_work(grad_mods):
        return [gather_rows(one[None], [("y", "x"), ("z",)]) for one in grad_mods]

    mods_of = overlap.alone(factor_work, [layer.grad_mod for layer in layers] + [grad_final])
    mods_of, final_of = mods_of[:LAYERS], mods_of[LAYERS]

    def grad_cond_work(grad_state, mods_of, final_of):
        grad_patch_b = jnp.sum(grad_state, axis=0)
        grad_patch_w = jnp.dot(patches.astype(F32), grad_state, precision=HIGH)
        once = jnp.where(c == 0, 1.0, 0.0)
        summed = jnp.concatenate(
            [grad_patch_w.reshape(-1) * once, grad_patch_b * once]
            + [layer.grad_bias for layer in layers]
            + [grad_head.reshape(-1) * once, jnp.pad(loss_part[None] * once, (0, 2 * LANE - 1))]
        )
        grad_cond = flat.back_product(held, mods_of + [final_of], adas + [final])
        return columns_by_core(summed), grad_cond, mods_of, final_of

    summed, grad_cond, mods_of, final_of = overlap.beside(
        grad_cond_work, grad_state, mods_of, final_of
    )
    grad_cond, mods_of, final_of = overlap.alone(
        lambda v, *more: (all_sum(v),) + more, grad_cond, mods_of, final_of
    )

    def grad_hidden_work(grad_cond, mods_of, final_of):
        grad_cond = jax.vjp(jax.nn.silu, cond)[1](grad_cond)[0]
        return flat.back_product(held, [grad_cond], [w2]), grad_cond, mods_of, final_of

    grad_hidden, grad_cond, mods_of, final_of = overlap.beside(
        grad_hidden_work, grad_cond, mods_of, final_of
    )

    def last_sums(summed, grad_hidden, grad_cond, mods_of, final_of):
        grad_hidden = all_sum(grad_hidden, stem_axes)
        grad_hidden = jax.vjp(jax.nn.silu, hidden_pre)[1](grad_hidden)[0]
        summed = columns_of_cores(all_sum(summed, (("y", "x"), ("z",))))
        return summed.reshape(-1, LANE), grad_hidden, grad_cond, mods_of, final_of

    summed, grad_hidden, grad_cond, mods_of, final_of = overlap.beside(
        last_sums, summed, grad_hidden, grad_cond, mods_of, final_of
    )
    stem_rows = summed[:ROW_STEM]
    extra = ROW_BIAS - ROW_ADA
    bias_rows = [summed[ROW_STEM + l * extra : ROW_STEM + (l + 1) * extra] for l in range(LAYERS)]
    head_rows = summed[ROW_STEM + LAYERS * extra : -2]
    summed_loss = summed[-2, 0]

    def total_rows(values):
        return jnp.sum(values, axis=0).reshape(-1, LANE)

    cond_f = cond_s.astype(F32)

    def flat_work(grad_hidden, grad_cond, mods_of, final_of):
        parts = [
            (0, stem_rows),
            (BASE_W1, ROW_D, freq, grad_hidden),
            (BASE_B1, total_rows(grad_hidden)),
            (BASE_W2, ROW_D, hidden, grad_cond),
            (BASE_B2, total_rows(grad_cond)),
            (BASE_TABLE, ROW_D, onehot, grad_cond),
        ]
        for layer in range(LAYERS):
            base = BASE_LAYER + layer * LAYER_ROWS
            parts.append((base, ROW_ADA, cond_f, mods_of[layer]))
            vector = jnp.concatenate([total_rows(mods_of[layer]), bias_rows[layer]])
            parts.append((base + D * ROW_ADA, vector))
        parts.append((BASE_FINAL, ROW_FINAL, cond_f, final_of))
        parts.append((BASE_TAIL, jnp.concatenate([total_rows(final_of), head_rows])))
        return flat.gradient(parts)

    grad_flat, square_flat = overlap.beside(flat_work, grad_hidden, grad_cond, mods_of, final_of)
    while overlap.source is not None:
        grad_flat, square_flat = overlap.beside(lambda *v: v, grad_flat, square_flat)
    if simple:
        grad_tiles = tiles_of(by_plane(done)[None], is_mixer)
    else:
        grad_tiles = reduce_any(grad_planes, count_tiles)

    square = square_flat + jnp.sum(jnp.square(grad_tiles.astype(F32)))
    norm = jnp.sqrt(all_sum(square.reshape(1, 1))[0, 0])
    factor = jnp.minimum(1.0, CLIP_AT / (norm + 1e-06))
    new_moment, new_second, new_flat = adamw(
        grad_flat * factor, flat_moment, flat_second, flat_master
    )
    tile_mom, new_left, new_right, new_tiles = shampoo(
        factor,
        grad_tiles,
        tile_moment[0],
        tile_left[0],
        tile_right[0],
        left_root[0],
        right_root[0],
        tile_master[0],
    )
    return (
        summed_loss,
        count,
        norm,
        new_moment,
        new_second,
        new_flat,
        tile_mom[None],
        new_left[None],
        new_right[None],
        new_tiles[None],
    )


def solution(mesh):
    deep = 4
    axes = Mesh(
        mesh.devices.reshape(deep, mesh.shape["dp"] // deep, MB, mesh.shape["mp"] // MB),
        ("z", "y", "x", "c"),
    )
    dp, mp, whole = ("z", "y"), ("x", "c"), ("z", "y", "x", "c")
    tile = P(mp, dp, None, None)
    in_specs = (
        P(None, None, whole),
        P(None, None, whole),
        P(None, dp),
        P(None, dp),
        P(None, None, dp),
        P(whole),
        P(whole),
        P(whole),
    ) + (tile,) * 6
    out_specs = (P(), P(), P(), P(whole), P(whole), P(whole)) + (tile,) * 4
    return jax.shard_map(local, mesh=axes, in_specs=in_specs, out_specs=out_specs, check_vma=False)
```

time: 1910 us -> 1500 us (0.79)
  Pallas kernels: 0 us -> 439 us
  waiting for transfers between devices: 616 us -> 239 us
  local copies, waits for them, and re-layouts: 378 us -> 125 us
  matrix products: 411 us -> 243 us
  other arithmetic: 313 us -> 257 us
    pallas_call x0 -> x18, Pallas kernels: none -> 439 us  [the longest x1 292 us: gather_strips(): pl.pallas_call(gather_kernel, out_shape=jax.ShapeDtypeStruct((2, 8 * STRI...]
    ppermute x111 -> x118, waiting for transfers between devices: 615 us -> 225 us  [the longest x40 188 us: beside(): lax.ppermute(value, move[1], move[2])]
    dot_general x93 -> x19, matrix products: 279 us -> 83.4 us  [the longest x4 32 us: widen_one(): pre = jnp.dot(normed, self.up_w[i], preferred_element_type=F32) + bias]
    dynamic_update_slice x39 -> x0, local copies, waits for them, and re-layouts: 175 us -> none  [the longest x16 97.7 us: attend_forward(): lax.map(one_block, query.reshape(rows // block, block, heads, HD))]
    reshape x19 -> x8, local copies, waits for them, and re-layouts: 44.7 us -> 6.18 us  [the longest x2 3.02 us: columns_by_core(): parts = value.reshape(value.shape[:-1] + (2, -1))]
    add x32 -> x23, other arithmetic: 9.73 us -> 37.3 us  [the longest x13 11.7 us: tree_sum(): values = [values[i] + values[i + 1] for i in range(0, len(values), 2)]]
    convert_element_type x20 -> x6, other arithmetic: 31.9 us -> 7.37 us  [the longest x2 3.96 us: mix_first(): normed = modulate(state, self.shift_a, self.scale_a).astype(BF16)]
    select_n x18 -> x15, other arithmetic: 30.5 us -> 7.19 us  [the longest x1 5.83 us: by_plane(): chosen = value if chosen is None else jnp.where(z == place, value, chosen)]
  transfers between devices with their start and end apart: 123 -> 130, of which waited for: 53 -> 42; matrix products, arithmetic and copies ran while one was open for 42% -> 17% of each run, Pallas kernels for 0% -> 6%
where the time goes in v1:
time: 1500 us; the launch traced here: 1490 us
  Pallas kernels  439 us (29%)
  other arithmetic  257 us (17%)
  matrix products  243 us (16%)
  waiting for transfers between devices  239 us (16%)
  starting transfers between devices  170 us (11%)
  local copies, waits for them, and re-layouts  125 us (8%)
  between operations  17.2 us (1%)
    pallas_call x1, Pallas kernels, gather_strips(): pl.pallas_call(gather_kernel, out_shape=jax.ShapeDtypeStruct((2, 8 * STRI...  292 us
    ppermute x40, waiting for transfers between devices, beside(): lax.ppermute(value, move[1], move[2])  188 us
    ppermute x74, starting transfers between devices, from_others(): lax.ppermute(pick(k), axes, [(i, i ^ k) for i in range(size)])  101 us
    dot_general x17, matrix products, contract_cols(): lax.dot_general(left, right, (((1,), (1,)), ((), ())), preferred_element_...  89.1 us
    dot_general x18, matrix products, contract_rows(): lax.dot_general(left, right, (((0,), (0,)), ((), ())), preferred_element_...  68.8 us
    ppermute x40, starting transfers between devices, beside(): lax.ppermute(value, move[1], move[2])  65.4 us
    convert_element_type x28, other arithmetic, add_low(): return (left.astype(F32) + right.astype(F32)).astype(BF16)  57.6 us
    pallas_call x4, Pallas kernels, attend_back(): pl.pallas_call(functools.partial(attend_back_kernel, block), out_shape=ja...  52 us
  transfers between devices with their start and end apart: 130, of which 42 were waited for; matrix products, arithmetic and copies ran while one was open for 17% of the time, Pallas kernels for 6%

profile of v1, /device:TPU:0, one launch (start us, length us, event | category | flops | bytes accessed | tf_op | source)
XLA Modules:
  0.0 1489.8 jit_solution(8821869024775215922)
XLA Ops:
  2.4 6.0 collective-permute-start.14
  19.1 5.0 copy.257
  24.1 5.0 bitcast_select_fusion.2
  29.1 5.5 select_n.483.strip_ref
  37.2 5.2 align.1.refs_0_
  166.5 5.0 collective-permute-done.33
  178.1 4.9 fusion
  183.9 291.7 %gather_strips.1 = bf16[2,6912,1152]{2,1,0:T(8,128)(2,1)} custom-call(bf16[864,1152]{1,0:T(8,128)(2,1)} %select_n.483.strip_ref), custom_call_target="tpu_custom_call" | custom-call | tf_op jit(solution)/shard_map/gather_strips/pallas_call | solution.py:467
  485.0 4.9 add_convert_fusion.14.mixed_ref
  489.9 7.6 attend.4
  502.9 7.7 attend.5
  520.9 6.3 multiply_add_fusion.3
  534.4 7.9 fusion.36
  542.3 7.9 fusion.44
  550.3 6.1 fusion.89
  556.4 5.8 add_convert_fusion.8
  566.9 6.2 multiply_add_fusion.2
  580.4 4.9 add_convert_fusion.12.mixed_ref
  585.3 7.5 attend.6
  598.1 8.0 attend.7
  627.9 8.0 fusion.52
  635.9 8.1 fusion.60
  644.0 6.1 fusion.73
  650.2 6.6 add_convert_fusion.5
  661.6 4.9 fusion.226
  673.9 6.1 multiply_reduce_fusion.23
  680.1 4.8 convolution_convert_fusion.4
  689.6 6.9 fusion.14
  696.6 9.4 fusion.7
  716.6 5.6 fusion.79
  722.2 5.9 add_convert_fusion.3
  754.7 5.7 multiply_reduce_fusion.22
  763.1 13.1 attend_back.4
  778.0 16.5 %collective-permute-done.44 = bf16[2,432,1152]{2,1,0:T(8,128)(2,1)} collective-permute-done((bf16[2,432,1152]{2,1,0:T(8,128)(2,1)}, bf16[2,432,1152]{2,1,0:T(8,128)(2,1)}, u32[]{:S(2)}, u32[]{:S(2)}) %collective-permute-start.44) | collective-permute-done | bytes 1990688 | tf_op jit(solution)/shard_map/ppermute | solution.py:242
  807.9 13.3 attend_back.5
  834.6 6.0 fusion.133
  844.0 5.6 add_convert_fusion.2
  878.4 8.6 fusion.28
  887.0 7.7 fusion.21
  901.4 5.4 collective-permute-start.53
  909.9 14.9 %collective-permute-done.53 = bf16[432,1152]{1,0:T(8,128)(2,1)S(1)} collective-permute-done((bf16[432,1152]{1,0:T(8,128)(2,1)S(1)}, bf16[432,1152]{1,0:T(8,128)(2,1)S(1)}, u32[]{:S(2)}, u32[]{:S(2)}) %collective-permute-start.53) | collective-permute-done | bytes 995360 | tf_op jit(solution)/shard_map/ppermute | solution.py:242
  926.0 12.1 collective-permute-done.51
  939.7 9.1 collective-permute-done.50
  958.3 7.9 fusion.93
  973.0 7.4 add_convert_fusion.1
  1006.2 10.0 collective-permute-start.62
  1026.6 12.8 attend_back.6
  1050.4 10.6 collective-permute-done.59
  1075.6 12.8 attend_back.7
  1100.1 6.1 fusion.140
  1112.7 5.7 add_convert_fusion
  1198.4 10.7 collective-permute-done.93
  1209.1 15.9 %collective-permute-done.91 = bf16[2,432,1152]{2,1,0:T(8,128)(2,1)} collective-permute-done((bf16[2,432,1152]{2,1,0:T(8,128)(2,1)}, bf16[2,432,1152]{2,1,0:T(8,128)(2,1)}, u32[]{:S(2)}, u32[]{:S(2)}) %collective-permute-start.91) | collective-permute-done | bytes 1990688 | tf_op jit(solution)/shard_map/ppermute | solution.py:242
  1258.7 5.2 back_product.3
  1264.9 13.4 collective-permute-done.103
  1278.9 5.1 add_convert_fusion.26
  1318.4 8.8 flat_gradient.1
  1335.1 45.3 %collective-permute-done.120 = bf16[432,1152]{1,0:T(8,128)(2,1)S(1)} collective-permute-done((bf16[432,1152]{1,0:T(8,128)(2,1)S(1)}, bf16[432,1152]{1,0:T(8,128)(2,1)S(1)}, u32[]{:S(2)}, u32[]{:S(2)}) %collective-permute-start.120) | collective-permute-done | bytes 995360 | tf_op jit(solution)/shard_map/ppermute | solution.py:242
  1382.9 20.6 %collective-permute-done.122 = bf16[432,1152]{1,0:T(8,128)(2,1)S(1)} collective-permute-done((bf16[432,1152]{1,0:T(8,128)(2,1)S(1)}, bf16[432,1152]{1,0:T(8,128)(2,1)S(1)}, u32[]{:S(2)}, u32[]{:S(2)}) %collective-permute-start.122) | collective-permute-done | bytes 995360 | tf_op jit(solution)/shard_map/ppermute | solution.py:242
  1403.9 5.8 maximum_select_fusion
  1409.7 5.1 select_n.579
  1416.6 5.0 copy.325
  1451.8 8.7 multiply_subtract_fusion
  1460.5 27.7 %shampoo.1 = (f32[12,288,288]{2,1,0:T(8,128)}, f32[12,288,288]{2,1,0:T(8,128)}, f32[12,288,288]{2,1,0:T(8,128)}, f32[12,288,288]{2,1,0:T(8,128)}) custom-call(f32[1]{0:T(128)} %bitcast.151.factor, bf16[12,288,288]{2,1,0:T(8,128)(2,1)S(1)} %bitcast_select_fusion.grad, f32[12,288,288]{2,1,0:T(8,128)} %bitcast.551, f32[12,288,288]{2,1,0:T(8,128)} %bitcast.552, ...), custom_call_target="tpu_custom_call" | custom-call | tf_op jit(solution)/shard_map/shampoo/pallas_call | solution.py:1174
  (1165 shorter events, 622.7 us)
Async XLA Ops:
  2.4 50.1 %collective-permute-start.14 = (s32[1,4,2]{2,1,0:T(4,128)S(1)}, s32[1,4,2]{2,1,0:T(4,128)S(1)}, u32[]{:S(2)}, u32[]{:S(2)}) collective-permute-start(s32[1,4,2]{2,1,0:T(4,128)S(1)} %reshape.785), channel_id=1, source_target_pairs={{0,28},{4,24},{8,20},{12,16},{16,12},{20,8},{24,4},{28,0},{1,29},{... | collective-permute-start | bytes 104 | tf_op jit(solution)/shard_map/ppermute | solution.py:126
  8.4 44.0 %collective-permute-start.13 = (s32[1,4,2]{2,1,0:T(4,128)S(1)}, s32[1,4,2]{2,1,0:T(4,128)S(1)}, u32[]{:S(2)}, u32[]{:S(2)}) collective-permute-start(s32[1,4,2]{2,1,0:T(4,128)S(1)} %reshape.785), channel_id=1, source_target_pairs={{0,24},{4,28},{8,16},{12,20},{16,8},{20,12},{24,0},{28,4},{1,25},{... | collective-permute-start | bytes 104 | tf_op jit(solution)/shard_map/ppermute | solution.py:126
  8.7 43.8 %collective-permute-start.12 = (s32[1,4,2]{2,1,0:T(4,128)S(1)}, s32[1,4,2]{2,1,0:T(4,128)S(1)}, u32[]{:S(2)}, u32[]{:S(2)}) collective-permute-start(s32[1,4,2]{2,1,0:T(4,128)S(1)} %reshape.785), channel_id=1, source_target_pairs={{0,20},{4,16},{8,28},{12,24},{16,4},{20,0},{24,12},{28,8},{1,21},{... | collective-permute-start | bytes 104 | tf_op jit(solution)/shard_map/ppermute | solution.py:126
  9.4 42.5 %collective-permute-start.11 = (s32[1,4,2]{2,1,0:T(4,128)S(1)}, s32[1,4,2]{2,1,0:T(4,128)S(1)}, u32[]{:S(2)}, u32[]{:S(2)}) collective-permute-start(s32[1,4,2]{2,1,0:T(4,128)S(1)} %reshape.785), channel_id=1, source_target_pairs={{0,16},{4,20},{8,24},{12,28},{16,0},{20,4},{24,8},{28,12},{1,17},{... | collective-permute-start | bytes 104 | tf_op jit(solution)/shard_map/ppermute | solution.py:126
  11.4 30.9 %collective-permute-start.8 = (s32[1,4,2]{2,1,0:T(4,128)S(1)}, s32[1,4,2]{2,1,0:T(4,128)S(1)}, u32[]{:S(2)}, u32[]{:S(2)}) collective-permute-start(s32[1,4,2]{2,1,0:T(4,128)S(1)} %reshape.785), channel_id=1, source_target_pairs={{0,4},{4,0},{8,12},{12,8},{16,20},{20,16},{24,28},{28,24},{1,5},{5... | collective-permute-start | bytes 104 | tf_op jit(solution)/shard_map/ppermute | solution.py:126
  69.3 11.9 collective-permute-start.19
  82.0 21.1 %collective-permute-start.4 = (bf16[603,128]{1,0:T(8,128)(2,1)}, bf16[603,128]{1,0:T(8,128)(2,1)}, u32[]{:S(2)}, u32[]{:S(2)}) collective-permute-start(bf16[603,128]{1,0:T(8,128)(2,1)} %slice.507), channel_id=1, source_target_pairs={{0,1},{1,0},{2,3},{3,2},{4,5},{5,4},{6,7},{7,6},{8,9},{9,8},{10,11... | collective-permute-start | bytes 463112 | tf_op jit(solution)/shard_map/ppermute | solution.py:126
  98.0 11.8 collective-permute-start.24
  116.6 17.4 %collective-permute-start.30 = (f32[16,1152]{1,0:T(8,128)}, f32[16,1152]{1,0:T(8,128)S(1)}, u32[]{:S(2)}, u32[]{:S(2)}) collective-permute-start(f32[16,1152]{1,0:T(8,128)} %copy.290), channel_id=1, source_target_pairs={{0,24},{8,16},{16,8},{24,0},{1,25},{9,17},{17,9},{25,1},{2,26},{10... | collective-permute-start | bytes 221192 | tf_op jit(solution)/shard_map/ppermute | solution.py:126
  117.6 14.5 collective-permute-start.29
  121.0 15.8 %collective-permute-start.27 = (bf16[603,128]{1,0:T(8,128)(2,1)}, bf16[603,128]{1,0:T(8,128)(2,1)}, u32[]{:S(2)}, u32[]{:S(2)}) collective-permute-start(bf16[603,128]{1,0:T(8,128)(2,1)} %add_add_fusion.19), channel_id=1, source_target_pairs={{0,24},{8,16},{16,8},{24,0},{1,25},{9,17},{17,9},{25,1},{2,26},{10... | collective-permute-start | bytes 463112 | tf_op jit(solution)/shard_map/ppermute | solution.py:126
  122.1 17.0 %collective-permute-start.26 = (bf16[603,128]{1,0:T(8,128)(2,1)}, bf16[603,128]{1,0:T(8,128)(2,1)}, u32[]{:S(2)}, u32[]{:S(2)}) collective-permute-start(bf16[603,128]{1,0:T(8,128)(2,1)} %add_add_fusion.19), channel_id=1, source_target_pairs={{0,16},{8,24},{16,0},{24,8},{1,17},{9,25},{17,1},{25,9},{2,18},{10... | collective-permute-start | bytes 463112 | tf_op jit(solution)/shard_map/ppermute | solution.py:126
  125.3 13.7 collective-permute-start.25
  728.1 12.9 collective-permute-start.43
  748.6 45.9 %collective-permute-start.44 = (bf16[2,432,1152]{2,1,0:T(8,128)(2,1)}, bf16[2,432,1152]{2,1,0:T(8,128)(2,1)}, u32[]{:S(2)}, u32[]{:S(2)}) collective-permute-start(bf16[2,432,1152]{2,1,0:T(8,128)(2,1)} %pad_maximum_fusion), channel_id=1, source_target_pairs={{0,2},{2,0},{1,3},{3,1},{4,6},{6,4},{5,7},{7,5},{8,10},{10,8},{9,1... | collective-permute-start | bytes 5971976 | tf_op jit(solution)/shard_map/ppermute | solution.py:242
  753.4 45.6 %collective-permute-start.45 = (bf16[2,432,1152]{2,1,0:T(8,128)(2,1)}, bf16[2,432,1152]{2,1,0:T(8,128)(2,1)}, u32[]{:S(2)}, u32[]{:S(2)}) collective-permute-start(bf16[2,432,1152]{2,1,0:T(8,128)(2,1)} %pad_maximum_fusion.1), channel_id=1, source_target_pairs={{0,4},{4,0},{1,5},{5,1},{2,6},{6,2},{3,7},{7,3},{8,12},{12,8},{9,1... | collective-permute-start | bytes 5971976 | tf_op jit(solution)/shard_map/ppermute | solution.py:242
  801.8 23.4 %collective-permute-start.46 = (bf16[432,1152]{1,0:T(8,128)(2,1)}, bf16[432,1152]{1,0:T(8,128)(2,1)S(1)}, u32[]{:S(2)}, u32[]{:S(2)}) collective-permute-start(bf16[432,1152]{1,0:T(8,128)(2,1)} %broadcast_select_fusion.3), channel_id=1, source_target_pairs={{0,4},{4,0},{1,5},{5,1},{2,6},{6,2},{3,7},{7,3},{8,12},{12,8},{9,1... | collective-permute-start | bytes 2985992 | tf_op jit(solution)/shard_map/ppermute | solution.py:242
  803.2 23.2 %collective-permute-start.47 = (bf16[432,1152]{1,0:T(8,128)(2,1)}, bf16[432,1152]{1,0:T(8,128)(2,1)}, u32[]{:S(2)}, u32[]{:S(2)}) collective-permute-start(bf16[432,1152]{1,0:T(8,128)(2,1)} %fusion.127), channel_id=1, source_target_pairs={{0,2},{2,0},{1,3},{3,1},{4,6},{6,4},{5,7},{7,5},{8,10},{10,8},{9,1... | collective-permute-start | bytes 2985992 | tf_op jit(solution)/shard_map/ppermute | solution.py:242
  842.3 21.6 %collective-permute-start.48 = (bf16[432,1152]{1,0:T(8,128)(2,1)}, bf16[432,1152]{1,0:T(8,128)(2,1)S(1)}, u32[]{:S(2)}, u32[]{:S(2)}) collective-permute-start(bf16[432,1152]{1,0:T(8,128)(2,1)} %get-tuple-element.192), channel_id=1, source_target_pairs={{0,8},{1,9},{2,10},{3,11},{4,12},{5,13},{6,14},{7,15}} | collective-permute-start | bytes 2985992 | tf_op jit(solution)/shard_map/ppermute | solution.py:242
  849.6 14.5 collective-permute-start.49
  894.8 13.8 collective-permute-start.52
  895.5 42.6 %collective-permute-start.51 = (bf16[2,432,1152]{2,1,0:T(8,128)(2,1)S(1)}, bf16[2,432,1152]{2,1,0:T(8,128)(2,1)S(1)}, u32[]{:S(2)}, u32[]{:S(2)}) collective-permute-start(bf16[2,432,1152]{2,1,0:T(8,128)(2,1)S(1)} %copy-done.136), channel_id=1, source_target_pairs={{0,4},{4,0},{1,5},{5,1},{2,6},{6,2},{3,7},{7,3},{8,12},{12,8},{9,1... | collective-permute-start | bytes 5971976 | tf_op jit(solution)/shard_map/ppermute | solution.py:242
  901.4 23.3 %collective-permute-start.53 = (bf16[432,1152]{1,0:T(8,128)(2,1)S(1)}, bf16[432,1152]{1,0:T(8,128)(2,1)S(1)}, u32[]{:S(2)}, u32[]{:S(2)}) collective-permute-start(bf16[432,1152]{1,0:T(8,128)(2,1)S(1)} %copy-done.94), channel_id=1, source_target_pairs={{0,8},{1,9},{2,10},{3,11},{4,12},{5,13},{6,14},{7,15}} | collective-permute-start | bytes 2985992 | tf_op jit(solution)/shard_map/ppermute | solution.py:242
  906.8 42.0 %collective-permute-start.50 = (bf16[2,432,1152]{2,1,0:T(8,128)(2,1)S(1)}, bf16[2,432,1152]{2,1,0:T(8,128)(2,1)S(1)}, u32[]{:S(2)}, u32[]{:S(2)}) collective-permute-start(bf16[2,432,1152]{2,1,0:T(8,128)(2,1)S(1)} %copy-done.135), channel_id=1, source_target_pairs={{0,2},{2,0},{1,3},{3,1},{4,6},{6,4},{5,7},{7,5},{8,10},{10,8},{9,1... | collective-permute-start | bytes 5971976 | tf_op jit(solution)/shard_map/ppermute | solution.py:242
  969.0 22.5 %collective-permute-start.54 = (bf16[432,1152]{1,0:T(8,128)(2,1)}, bf16[432,1152]{1,0:T(8,128)(2,1)S(1)}, u32[]{:S(2)}, u32[]{:S(2)}) collective-permute-start(bf16[432,1152]{1,0:T(8,128)(2,1)} %broadcast_select_fusion.2), channel_id=1, source_target_pairs={{0,4},{4,0},{1,5},{5,1},{2,6},{6,2},{3,7},{7,3},{8,12},{12,8},{9,1... | collective-permute-start | bytes 2985992 | tf_op jit(solution)/shard_map/ppermute | solution.py:242
  970.4 21.1 %collective-permute-start.55 = (bf16[432,1152]{1,0:T(8,128)(2,1)}, bf16[432,1152]{1,0:T(8,128)(2,1)S(1)}, u32[]{:S(2)}, u32[]{:S(2)}) collective-permute-start(bf16[432,1152]{1,0:T(8,128)(2,1)} %fusion.123), channel_id=1, source_target_pairs={{0,2},{2,0},{1,3},{3,1},{4,6},{6,4},{5,7},{7,5},{8,10},{10,8},{9,1... | collective-permute-start | bytes 2985992 | tf_op jit(solution)/shard_map/ppermute | solution.py:242
  971.4 31.5 %collective-permute-start.56 = (bf16[432,1152]{1,0:T(8,128)(2,1)}, bf16[432,1152]{1,0:T(8,128)(2,1)S(1)}, u32[]{:S(2)}, u32[]{:S(2)}) collective-permute-start(bf16[432,1152]{1,0:T(8,128)(2,1)} %add_convert_fusion.43), channel_id=1, source_target_pairs={{16,24},{17,25},{18,26},{19,27},{20,28},{21,29},{22,30},{23,31}} | collective-permute-start | bytes 2985992 | tf_op jit(solution)/shard_map/ppermute | solution.py:242
  972.1 17.3 %collective-permute-start.57 = (bf16[432,1152]{1,0:T(8,128)(2,1)}, bf16[432,1152]{1,0:T(8,128)(2,1)S(1)}, u32[]{:S(2)}, u32[]{:S(2)}) collective-permute-start(bf16[432,1152]{1,0:T(8,128)(2,1)} %add_convert_fusion.42), channel_id=1, source_target_pairs={{8,16},{9,17},{10,18},{11,19},{12,20},{13,21},{14,22},{15,23}} | collective-permute-start | bytes 2985992 | tf_op jit(solution)/shard_map/ppermute | solution.py:242
  980.5 14.8 collective-permute-start.58
  1003.0 44.7 %collective-permute-start.60 = (bf16[2,432,1152]{2,1,0:T(8,128)(2,1)}, bf16[2,432,1152]{2,1,0:T(8,128)(2,1)}, u32[]{:S(2)}, u32[]{:S(2)}) collective-permute-start(bf16[2,432,1152]{2,1,0:T(8,128)(2,1)} %pad_maximum_fusion.5), channel_id=1, source_target_pairs={{0,4},{4,0},{1,5},{5,1},{2,6},{6,2},{3,7},{7,3},{8,12},{12,8},{9,1... | collective-permute-start | bytes 5971976 | tf_op jit(solution)/shard_map/ppermute | solution.py:242
  1004.6 57.9 %collective-permute-start.61 = (bf16[432,1152]{1,0:T(8,128)(2,1)}, bf16[432,1152]{1,0:T(8,128)(2,1)}, u32[]{:S(2)}, u32[]{:S(2)}) collective-permute-start(bf16[432,1152]{1,0:T(8,128)(2,1)} %add_convert_fusion.41), channel_id=1, source_target_pairs={{16,24},{17,25},{18,26},{19,27},{20,28},{21,29},{22,30},{23,31}} | collective-permute-start | bytes 2985992 | tf_op jit(solution)/shard_map/ppermute | solution.py:242
  1006.2 33.2 %collective-permute-start.62 = (bf16[432,1152]{1,0:T(8,128)(2,1)}, bf16[432,1152]{1,0:T(8,128)(2,1)S(1)}, u32[]{:S(2)}, u32[]{:S(2)}) collective-permute-start(bf16[432,1152]{1,0:T(8,128)(2,1)} %get-tuple-element.212), channel_id=1, source_target_pairs={{0,8},{1,9},{2,10},{3,11},{4,12},{5,13},{6,14},{7,15}} | collective-permute-start | bytes 2985992 | tf_op jit(solution)/shard_map/ppermute | solution.py:242
  1016.3 24.2 %collective-permute-start.63 = (bf16[432,1152]{1,0:T(8,128)(2,1)}, bf16[432,1152]{1,0:T(8,128)(2,1)}, u32[]{:S(2)}, u32[]{:S(2)}) collective-permute-start(bf16[432,1152]{1,0:T(8,128)(2,1)} %get-tuple-element.212), channel_id=1, source_target_pairs={{24,16},{25,17},{26,18},{27,19},{28,20},{29,21},{30,22},{31,23}} | collective-permute-start | bytes 2985992 | tf_op jit(solution)/shard_map/ppermute | solution.py:242
  1018.1 43.0 %collective-permute-start.59 = (bf16[2,432,1152]{2,1,0:T(8,128)(2,1)}, bf16[2,432,1152]{2,1,0:T(8,128)(2,1)S(1)}, u32[]{:S(2)}, u32[]{:S(2)}) collective-permute-start(bf16[2,432,1152]{2,1,0:T(8,128)(2,1)} %pad_maximum_fusion.4), channel_id=1, source_target_pairs={{0,2},{2,0},{1,3},{3,1},{4,6},{6,4},{5,7},{7,5},{8,10},{10,8},{9,1... | collective-permute-start | bytes 5971976 | tf_op jit(solution)/shard_map/ppermute | solution.py:242
  1062.5 25.9 %collective-permute-start.67 = (bf16[432,1152]{1,0:T(8,128)(2,1)}, bf16[432,1152]{1,0:T(8,128)(2,1)}, u32[]{:S(2)}, u32[]{:S(2)}) collective-permute-start(bf16[432,1152]{1,0:T(8,128)(2,1)} %get-tuple-element.219), channel_id=1, source_target_pairs={{0,8},{1,9},{2,10},{3,11},{4,12},{5,13},{6,14},{7,15}} | collective-permute-start | bytes 2985992 | tf_op jit(solution)/shard_map/ppermute | solution.py:242
  1065.2 23.3 %collective-permute-start.68 = (bf16[432,1152]{1,0:T(8,128)(2,1)}, bf16[432,1152]{1,0:T(8,128)(2,1)}, u32[]{:S(2)}, u32[]{:S(2)}) collective-permute-start(bf16[432,1152]{1,0:T(8,128)(2,1)} %get-tuple-element.219), channel_id=1, source_target_pairs={{24,16},{25,17},{26,18},{27,19},{28,20},{29,21},{30,22},{31,23}} | collective-permute-start | bytes 2985992 | tf_op jit(solution)/shard_map/ppermute | solution.py:242
  1068.9 22.9 %collective-permute-start.64 = (bf16[432,1152]{1,0:T(8,128)(2,1)}, bf16[432,1152]{1,0:T(8,128)(2,1)}, u32[]{:S(2)}, u32[]{:S(2)}) collective-permute-start(bf16[432,1152]{1,0:T(8,128)(2,1)} %broadcast_select_fusion.1), channel_id=1, source_target_pairs={{0,4},{4,0},{1,5},{5,1},{2,6},{6,2},{3,7},{7,3},{8,12},{12,8},{9,1... | collective-permute-start | bytes 2985992 | tf_op jit(solution)/shard_map/ppermute | solution.py:242
  1070.0 21.8 %collective-permute-start.65 = (bf16[432,1152]{1,0:T(8,128)(2,1)}, bf16[432,1152]{1,0:T(8,128)(2,1)}, u32[]{:S(2)}, u32[]{:S(2)}) collective-permute-start(bf16[432,1152]{1,0:T(8,128)(2,1)} %fusion.120), channel_id=1, source_target_pairs={{0,2},{2,0},{1,3},{3,1},{4,6},{6,4},{5,7},{7,5},{8,10},{10,8},{9,1... | collective-permute-start | bytes 2985992 | tf_op jit(solution)/shard_map/ppermute | solution.py:242
  1070.8 25.2 %collective-permute-start.66 = (bf16[432,1152]{1,0:T(8,128)(2,1)S(1)}, bf16[432,1152]{1,0:T(8,128)(2,1)}, u32[]{:S(2)}, u32[]{:S(2)}) collective-permute-start(bf16[432,1152]{1,0:T(8,128)(2,1)S(1)} %add_convert_fusion.38), channel_id=1, source_target_pairs={{8,16},{9,17},{10,18},{11,19},{12,20},{13,21},{14,22},{15,23}} | collective-permute-start | bytes 2985992 | tf_op jit(solution)/shard_map/ppermute | solution.py:242
  1106.9 19.3 %collective-permute-start.69 = (bf16[432,1152]{1,0:T(8,128)(2,1)}, bf16[432,1152]{1,0:T(8,128)(2,1)S(1)}, u32[]{:S(2)}, u32[]{:S(2)}) collective-permute-start(bf16[432,1152]{1,0:T(8,128)(2,1)} %get-tuple-element.225), channel_id=1, source_target_pairs={{0,8},{1,9},{2,10},{3,11},{4,12},{5,13},{6,14},{7,15}} | collective-permute-start | bytes 2985992 | tf_op jit(solution)/shard_map/ppermute | solution.py:242
  1109.2 17.0 %collective-permute-start.70 = (bf16[432,1152]{1,0:T(8,128)(2,1)}, bf16[432,1152]{1,0:T(8,128)(2,1)S(1)}, u32[]{:S(2)}, u32[]{:S(2)}) collective-permute-start(bf16[432,1152]{1,0:T(8,128)(2,1)} %get-tuple-element.225), channel_id=1, source_target_pairs={{24,16},{25,17},{26,18},{27,19},{28,20},{29,21},{30,22},{31,23}} | collective-permute-start | bytes 2985992 | tf_op jit(solution)/shard_map/ppermute | solution.py:242
  1110.0 20.2 %collective-permute-start.72 = (bf16[432,1152]{1,0:T(8,128)(2,1)}, bf16[432,1152]{1,0:T(8,128)(2,1)S(1)}, u32[]{:S(2)}, u32[]{:S(2)}) collective-permute-start(bf16[432,1152]{1,0:T(8,128)(2,1)} %add_convert_fusion.35), channel_id=1, source_target_pairs={{8,16},{9,17},{10,18},{11,19},{12,20},{13,21},{14,22},{15,23}} | collective-permute-start | bytes 2985992 | tf_op jit(solution)/shard_map/ppermute | solution.py:242
  1132.8 11.5 collective-permute-start.85
  1147.0 11.7 collective-permute-start.90
  1148.2 11.9 collective-permute-start.89
  1157.0 15.1 %collective-permute-start.83 = (f32[4,6912]{1,0:T(4,128)S(1)}, f32[4,6912]{1,0:T(4,128)S(1)}, u32[]{:S(2)}, u32[]{:S(2)}) collective-permute-start(f32[4,6912]{1,0:T(4,128)S(1)} %reshape_reshape.53), channel_id=1, source_target_pairs={{0,16},{8,24},{16,0},{24,8},{1,17},{9,25},{17,1},{25,9},{2,18},{10... | collective-permute-start | bytes 331784 | tf_op jit(solution)/shard_map/ppermute | solution.py:126
  1158.6 13.5 collective-permute-start.82
  1160.1 12.5 collective-permute-start.78
  1161.4 13.0 collective-permute-start.77
  1181.6 43.3 %collective-permute-start.91 = (bf16[2,432,1152]{2,1,0:T(8,128)(2,1)}, bf16[2,432,1152]{2,1,0:T(8,128)(2,1)}, u32[]{:S(2)}, u32[]{:S(2)}) collective-permute-start(bf16[2,432,1152]{2,1,0:T(8,128)(2,1)} %pad_maximum_fusion.6), channel_id=1, source_target_pairs={{0,2},{2,0},{1,3},{3,1},{4,6},{6,4},{5,7},{7,5},{8,10},{10,8},{9,1... | collective-permute-start | bytes 5971976 | tf_op jit(solution)/shard_map/ppermute | solution.py:242
  1183.0 42.9 %collective-permute-start.92 = (bf16[2,432,1152]{2,1,0:T(8,128)(2,1)}, bf16[2,432,1152]{2,1,0:T(8,128)(2,1)}, u32[]{:S(2)}, u32[]{:S(2)}) collective-permute-start(bf16[2,432,1152]{2,1,0:T(8,128)(2,1)} %pad_maximum_fusion.7), channel_id=1, source_target_pairs={{0,4},{4,0},{1,5},{5,1},{2,6},{6,2},{3,7},{7,3},{8,12},{12,8},{9,1... | collective-permute-start | bytes 5971976 | tf_op jit(solution)/shard_map/ppermute | solution.py:242
  1185.1 23.9 %collective-permute-start.93 = (bf16[432,1152]{1,0:T(8,128)(2,1)}, bf16[432,1152]{1,0:T(8,128)(2,1)}, u32[]{:S(2)}, u32[]{:S(2)}) collective-permute-start(bf16[432,1152]{1,0:T(8,128)(2,1)} %get-tuple-element.233), channel_id=1, source_target_pairs={{0,8},{1,9},{2,10},{3,11},{4,12},{5,13},{6,14},{7,15}} | collective-permute-start | bytes 2985992 | tf_op jit(solution)/shard_map/ppermute | solution.py:242
  1187.5 21.5 %collective-permute-start.94 = (bf16[432,1152]{1,0:T(8,128)(2,1)}, bf16[432,1152]{1,0:T(8,128)(2,1)}, u32[]{:S(2)}, u32[]{:S(2)}) collective-permute-start(bf16[432,1152]{1,0:T(8,128)(2,1)} %get-tuple-element.233), channel_id=1, source_target_pairs={{24,16},{25,17},{26,18},{27,19},{28,20},{29,21},{30,22},{31,23}} | collective-permute-start | bytes 2985992 | tf_op jit(solution)/shard_map/ppermute | solution.py:242
  1189.1 19.9 %collective-permute-start.95 = (bf16[432,1152]{1,0:T(8,128)(2,1)}, bf16[432,1152]{1,0:T(8,128)(2,1)}, u32[]{:S(2)}, u32[]{:S(2)}) collective-permute-start(bf16[432,1152]{1,0:T(8,128)(2,1)} %add_convert_fusion.32), channel_id=1, source_target_pairs={{16,8},{17,9},{18,10},{19,11},{20,12},{21,13},{22,14},{23,15}} | collective-permute-start | bytes 2985992 | tf_op jit(solution)/shard_map/ppermute | solution.py:242
  1254.2 24.0 %collective-permute-start.103 = (bf16[432,1152]{1,0:T(8,128)(2,1)}, bf16[432,1152]{1,0:T(8,128)(2,1)}, u32[]{:S(2)}, u32[]{:S(2)}) collective-permute-start(bf16[432,1152]{1,0:T(8,128)(2,1)} %broadcast_select_fusion), channel_id=1, source_target_pairs={{0,4},{4,0},{1,5},{5,1},{2,6},{6,2},{3,7},{7,3},{8,12},{12,8},{9,1... | collective-permute-start | bytes 2985992 | tf_op jit(solution)/shard_map/ppermute | solution.py:242
  1255.2 23.7 %collective-permute-start.104 = (bf16[432,1152]{1,0:T(8,128)(2,1)}, bf16[432,1152]{1,0:T(8,128)(2,1)}, u32[]{:S(2)}, u32[]{:S(2)}) collective-permute-start(bf16[432,1152]{1,0:T(8,128)(2,1)} %fusion.115), channel_id=1, source_target_pairs={{0,2},{2,0},{1,3},{3,1},{4,6},{6,4},{5,7},{7,5},{8,10},{10,8},{9,1... | collective-permute-start | bytes 2985992 | tf_op jit(solution)/shard_map/ppermute | solution.py:242
  1263.9 20.1 %collective-permute-start.105 = (bf16[432,1152]{1,0:T(8,128)(2,1)S(1)}, bf16[432,1152]{1,0:T(8,128)(2,1)S(1)}, u32[]{:S(2)}, u32[]{:S(2)}) collective-permute-start(bf16[432,1152]{1,0:T(8,128)(2,1)S(1)} %copy-done.102), channel_id=1, source_target_pairs={{16,8},{17,9},{18,10},{19,11},{20,12},{21,13},{22,14},{23,15}} | collective-permute-start | bytes 2985992 | tf_op jit(solution)/shard_map/ppermute | solution.py:242
  1291.7 12.4 collective-permute-start.117
  1293.6 11.5 collective-permute-start.112
  1294.8 13.3 collective-permute-start.111
  1313.7 13.5 collective-permute-start.118
  1315.5 13.6 collective-permute-start.119
  1332.0 48.4 %collective-permute-start.120 = (bf16[432,1152]{1,0:T(8,128)(2,1)S(1)}, bf16[432,1152]{1,0:T(8,128)(2,1)S(1)}, u32[]{:S(2)}, u32[]{:S(2)}) collective-permute-start(bf16[432,1152]{1,0:T(8,128)(2,1)S(1)} %add_convert_fusion.25), channel_id=1, source_target_pairs={{8,0},{9,1},{10,2},{11,3},{12,4},{13,5},{14,6},{15,7}} | collective-permute-start | bytes 2985992 | tf_op jit(solution)/shard_map/ppermute | solution.py:242
  1380.4 23.2 %collective-permute-start.122 = (bf16[432,1152]{1,0:T(8,128)(2,1)S(1)}, bf16[432,1152]{1,0:T(8,128)(2,1)S(1)}, u32[]{:S(2)}, u32[]{:S(2)}) collective-permute-start(bf16[432,1152]{1,0:T(8,128)(2,1)S(1)} %add_convert_fusion.23), channel_id=1, source_target_pairs={{8,0},{9,1},{10,2},{11,3},{12,4},{13,5},{14,6},{15,7}} | collective-permute-start | bytes 2985992 | tf_op jit(solution)/shard_map/ppermute | solution.py:242
  (315 other events, 4026.5 us)
